TPU v7x, 32 devices: a whole 2x2x4 slice. The times are simulated.
32 devices in a mesh: dp: 8 (over y, x, core), pair: 4 (over z).
Axes of the slice: x: 2, y: 2, z: 4, core: 2. Of those that a mesh axis runs over, the one named last changes fastest.
Arguments:
- question_tokens: bfloat16 [256, 64, 768], P(('dp', 'pair')), may hold values from -6 to 6
- passage_tokens: bfloat16 [64, 256, 768], P(('dp', 'pair')), may hold values from -6 to 6
- passage_lengths: int32 [64, 4], P(('dp', 'pair')), may hold values from 1 to 128, 256 in all within a row
- positives: int32 [256], P(('dp', 'pair')), may hold values from 0 to 255
- attn_weight: float32 [2, 768, 3072], P(None, ('dp', 'pair'))
- attn_first: float32 [2, 768, 3072], P(None, ('dp', 'pair')), may hold values from -0.375 to 0.375
- attn_second: float32 [2, 768, 3072], P(None, ('dp', 'pair')), may hold values from 2.56e-05 to 0.0004096
- ffn_in_weight: float32 [2, 768, 3072], P(None, ('dp', 'pair')), may hold values from -0.21875 to 0.21875
- ffn_in_first: float32 [2, 768, 3072], P(None, ('dp', 'pair')), may hold values from -0.21875 to 0.21875
- ffn_in_second: float32 [2, 768, 3072], P(None, ('dp', 'pair')), may hold values from 9.216e-06 to 0.000147456
- ffn_out_weight: float32 [2, 3072, 768], P(None, ('dp', 'pair')), may hold values from -0.109375 to 0.109375
- ffn_out_first: float32 [2, 3072, 768], P(None, ('dp', 'pair')), may hold values from -0.5 to 0.5
- ffn_out_second: float32 [2, 3072, 768], P(None, ('dp', 'pair')), may hold values from 5.76e-05 to 0.0009216
- small_params: float32 [2, 9216], P(None, ('dp', 'pair'))
- small_first: float32 [2, 9216], P(None, ('dp', 'pair')), may hold values from -0.75 to 0.75
- small_second: float32 [2, 9216], P(None, ('dp', 'pair')), may hold values from 0.0001024 to 0.0016384
Outputs:
- attn_first_new: float32 [2, 768, 3072], P(None, ('dp', 'pair'))
- attn_second_new: float32 [2, 768, 3072], P(None, ('dp', 'pair'))
- attn_new: float32 [2, 768, 3072], P(None, ('dp', 'pair'))
- ffn_in_first_new: float32 [2, 768, 3072], P(None, ('dp', 'pair'))
- ffn_in_second_new: float32 [2, 768, 3072], P(None, ('dp', 'pair'))
- ffn_in_new: float32 [2, 768, 3072], P(None, ('dp', 'pair'))
- ffn_out_first_new: float32 [2, 3072, 768], P(None, ('dp', 'pair'))
- ffn_out_second_new: float32 [2, 3072, 768], P(None, ('dp', 'pair'))
- ffn_out_new: float32 [2, 3072, 768], P(None, ('dp', 'pair'))
- small_first_new: float32 [2, 9216], P(None, ('dp', 'pair'))
- small_second_new: float32 [2, 9216], P(None, ('dp', 'pair'))
- small_new: float32 [2, 9216], P(None, ('dp', 'pair'))
- question_grad: float32 [256, 64, 768], P(('dp', 'pair'))
- passage_grad: float32 [64, 256, 768], P(('dp', 'pair'))
Inputs may be any that keep to these rules, and one draw needn't show every extreme that they name: `passage_lengths`: each row's 4 passage lengths sum to 256, the longest in every row is 128.
All inputs are finite; a program needn't handle non-finite values.
Results may differ from a plain program's by a relative error of at most 0.014.
The roundings to bfloat16 on the way count: a program that leaves them out, or rounds other values in their place, can miss the bound.
Values may be sent and summed in bfloat16 or wider, within the bound.
A program may use at most 256 MiB of HBM per device.

v0:
```python
import jax
import jax.numpy as jnp
from jax import lax
from jax.sharding import PartitionSpec as P

HD = 64
STEP = 5


BETA_ONE = 0.9
BETA_TWO = 0.999
ADAM_EPS = 1e-08
NORM_EPS = 1e-06
RATE_MATRIX = 0.05
RATE_SMALL = 0.3
DECAY_MATRIX = 0.01


def layer_norm(values, norm_gain, norm_shift):
    row_mean = jnp.mean(values, axis=-1, keepdims=True)
    centred = values - row_mean
    spread = jnp.mean(centred * centred, axis=-1, keepdims=True)
    return centred * lax.rsqrt(spread + NORM_EPS) * norm_gain + norm_shift


def gelu_exact(values):
    return jax.nn.gelu(values, approximate=False)


def unpack(small_vec, model_width, hidden_width):
    widths = [model_width] * 5 + [hidden_width] + [model_width] * 3
    pieces = []
    offset = 0
    for length in widths:
        pieces.append(small_vec[offset : offset + length])
        offset = offset + length
    return pieces


def masked_scores(queries, key_rows, segment):
    scores = jnp.einsum(
        "blhe,bmhe->bhlm", queries, key_rows, preferred_element_type=jnp.float32
    ) * HD ** (-0.5)
    allowed = (segment[:, :, None] == segment[:, None, :])[:, None]
    return jnp.where(allowed, scores, -1000000000.0)


def encoder_forward(tokens, segment, attn_weights, inner_weight, outer_weight, small_vec):
    batch_size, length, model_width = tokens.shape
    head_count = model_width // HD
    flat_rows = tokens.reshape(batch_size * length, model_width)
    (
        bias_query,
        bias_value,
        bias_out,
        gain_one,
        shift_one,
        bias_inner,
        bias_outer,
        gain_two,
        shift_two,
    ) = unpack(small_vec, model_width, inner_weight.shape[1])
    bias_proj = jnp.concatenate([bias_query, jnp.zeros_like(bias_query), bias_value])
    projected = (
        jnp.dot(flat_rows, attn_weights[:, : 3 * model_width], preferred_element_type=jnp.float32)
        + bias_proj
    )
    projected = projected.astype(jnp.bfloat16).reshape(batch_size, length, 3, head_count, HD)
    queries = projected[:, :, 0]
    key_rows = projected[:, :, 1]
    value_rows = projected[:, :, 2]
    scores = masked_scores(queries, key_rows, segment)
    top_score = jnp.max(scores, axis=-1, keepdims=True)
    raised = jnp.exp(scores - top_score)
    totals = jnp.sum(raised, axis=-1, keepdims=True)
    attn_probs = (raised / totals).astype(jnp.bfloat16)
    log_total = top_score + jnp.log(totals)
    mixed_heads = jnp.einsum(
        "bhlm,bmhe->blhe", attn_probs, value_rows, preferred_element_type=jnp.float32
    )
    mixed_flat = mixed_heads.astype(jnp.bfloat16).reshape(batch_size * length, model_width)
    attn_out = (
        jnp.dot(mixed_flat, attn_weights[:, 3 * model_width :], preferred_element_type=jnp.float32)
        + bias_out
    )
    residual_one = flat_rows.astype(jnp.float32) + attn_out
    normed_one = layer_norm(residual_one, gain_one, shift_one)
    pre_act = (
        jnp.dot(normed_one.astype(jnp.bfloat16), inner_weight, preferred_element_type=jnp.float32)
        + bias_inner
    )
    activated = gelu_exact(pre_act).astype(jnp.bfloat16)
    branch = jnp.dot(activated, outer_weight, preferred_element_type=jnp.float32) + bias_outer
    residual_two = normed_one + branch
    result = layer_norm(residual_two, gain_two, shift_two).reshape(batch_size, length, model_width)
    kept_values = (
        queries,
        key_rows,
        value_rows,
        log_total,
        mixed_flat,
        residual_one,
        normed_one,
        pre_act,
        activated,
        residual_two,
    )
    return (result, kept_values)


def encoder_backward(
    tokens, segment, attn_weights, inner_weight, outer_weight, small_vec, kept_values, grad_result
):
    batch_size, length, model_width = tokens.shape
    head_count = model_width // HD
    flat_rows = tokens.reshape(batch_size * length, model_width)
    (
        queries,
        key_rows,
        value_rows,
        log_total,
        mixed_flat,
        residual_one,
        normed_one,
        pre_act,
        activated,
        residual_two,
    ) = kept_values
    (
        bias_query,
        bias_value,
        bias_out,
        gain_one,
        shift_one,
        bias_inner,
        bias_outer,
        gain_two,
        shift_two,
    ) = unpack(small_vec, model_width, inner_weight.shape[1])
    grad_flat = grad_result.reshape(batch_size * length, model_width)
    unused_two, norm_two_back = jax.vjp(layer_norm, residual_two, gain_two, shift_two)
    grad_two, grad_gain_two, grad_shift_two = norm_two_back(grad_flat)
    grad_branch = grad_two.astype(jnp.bfloat16)
    grad_bias_outer = jnp.sum(grad_branch, axis=0, dtype=jnp.float32)
    grad_outer = jnp.dot(activated.T, grad_branch, preferred_element_type=jnp.float32)
    grad_act = jnp.dot(grad_branch, outer_weight.T, preferred_element_type=jnp.float32)
    unused_act, gelu_back = jax.vjp(gelu_exact, pre_act)
    grad_pre = gelu_back(grad_act)[0].astype(jnp.bfloat16)
    grad_bias_inner = jnp.sum(grad_pre, axis=0, dtype=jnp.float32)
    grad_inner = jnp.dot(
        normed_one.astype(jnp.bfloat16).T, grad_pre, preferred_element_type=jnp.float32
    )
    grad_normed = grad_two + jnp.dot(grad_pre, inner_weight.T, preferred_element_type=jnp.float32)
    unused_one, norm_one_back = jax.vjp(layer_norm, residual_one, gain_one, shift_one)
    grad_one, grad_gain_one, grad_shift_one = norm_one_back(grad_normed)
    grad_attn_out = grad_one.astype(jnp.bfloat16)
    grad_bias_out = jnp.sum(grad_attn_out, axis=0, dtype=jnp.float32)
    grad_out_proj = jnp.dot(mixed_flat.T, grad_attn_out, preferred_element_type=jnp.float32)
    grad_mixed = jnp.dot(
        grad_attn_out, attn_weights[:, 3 * model_width :].T, preferred_element_type=jnp.float32
    )
    grad_mixed = grad_mixed.astype(jnp.bfloat16).reshape(batch_size, length, head_count, HD)
    scores = masked_scores(queries, key_rows, segment)
    attn_probs = jnp.exp(scores - log_total)
    grad_probs = jnp.einsum(
        "blhe,bmhe->bhlm", grad_mixed, value_rows, preferred_element_type=jnp.float32
    )
    inner_dot = jnp.sum(attn_probs * grad_probs, axis=-1, keepdims=True)
    grad_scores = (attn_probs * (grad_probs - inner_dot)).astype(jnp.bfloat16)
    grad_values = jnp.einsum(
        "bhlm,blhe->bmhe",
        attn_probs.astype(jnp.bfloat16),
        grad_mixed,
        preferred_element_type=jnp.float32,
    )
    grad_queries = jnp.einsum(
        "bhlm,bmhe->blhe", grad_scores, key_rows, preferred_element_type=jnp.float32
    ) * HD ** (-0.5)
    grad_keys = jnp.einsum(
        "bhlm,blhe->bmhe", grad_scores, queries, preferred_element_type=jnp.float32
    ) * HD ** (-0.5)
    row_total = batch_size * length
    grad_proj = jnp.concatenate(
        [
            grad_queries.reshape(row_total, model_width),
            grad_keys.reshape(row_total, model_width),
            grad_values.reshape(row_total, model_width),
        ],
        axis=1,
    ).astype(jnp.bfloat16)
    grad_bias_query = jnp.sum(grad_proj[:, :model_width], axis=0, dtype=jnp.float32)
    grad_bias_value = jnp.sum(grad_proj[:, 2 * model_width :], axis=0, dtype=jnp.float32)
    grad_proj_weight = jnp.dot(flat_rows.T, grad_proj, preferred_element_type=jnp.float32)
    grad_tokens = grad_one + jnp.dot(
        grad_proj, attn_weights[:, : 3 * model_width].T, preferred_element_type=jnp.float32
    )
    grad_attn = jnp.concatenate([grad_proj_weight, grad_out_proj], axis=1)
    grad_small = jnp.concatenate(
        [
            grad_bias_query,
            grad_bias_value,
            grad_bias_out,
            grad_gain_one,
            grad_shift_one,
            grad_bias_inner,
            grad_bias_outer,
            grad_gain_two,
            grad_shift_two,
        ]
    )
    return (
        grad_tokens.reshape(batch_size, length, model_width),
        grad_attn,
        grad_inner,
        grad_outer,
        grad_small,
    )


def rows_term(stacked, count):
    return jnp.moveaxis(stacked, 0, 1).reshape(count, -1)


def unfold_rows(summed, encoders):
    owned = summed.shape[0]
    return jnp.moveaxis(summed.reshape(owned, encoders, -1), 1, 0)


def adam_update(weight, first_moment, second, gradient, step_rate, decay_rate):
    first_new = BETA_ONE * first_moment + (1.0 - BETA_ONE) * gradient
    second_new = BETA_TWO * second + (1.0 - BETA_TWO) * gradient * gradient
    fix_one = 1.0 - BETA_ONE**STEP
    fix_two = 1.0 - BETA_TWO**STEP
    update = first_new / fix_one / (jnp.sqrt(second_new / fix_two) + ADAM_EPS)
    return (first_new, second_new, weight - step_rate * (update + decay_rate * weight))


def local(
    question_tokens,
    passage_tokens,
    passage_lengths,
    positives,
    attn_weight,
    attn_first,
    attn_second,
    ffn_in_weight,
    ffn_in_first,
    ffn_in_second,
    ffn_out_weight,
    ffn_out_first,
    ffn_out_second,
    small_params,
    small_first,
    small_second,
):
    gathered = (
        lax.all_gather(attn_weight.astype(jnp.bfloat16), ("dp", "pair"), axis=1, tiled=True),
        lax.all_gather(ffn_in_weight.astype(jnp.bfloat16), ("dp", "pair"), axis=1, tiled=True),
        lax.all_gather(ffn_out_weight.astype(jnp.bfloat16), ("dp", "pair"), axis=1, tiled=True),
        lax.all_gather(small_params.astype(jnp.bfloat16), ("dp", "pair"), axis=1, tiled=True),
    )
    attn_all, inner_all, outer_all, small_low = gathered
    small_all = small_low.astype(jnp.float32)
    question_count, question_len, model_width = question_tokens.shape
    row_count, row_len, unused_width = passage_tokens.shape
    attn_cols = attn_weight.shape[2]
    front_rows = attn_weight.shape[1]
    back_rows = ffn_out_weight.shape[1]
    seg_ends = jnp.cumsum(passage_lengths, axis=1)
    seg_starts = seg_ends - passage_lengths
    positions = jnp.arange(row_len, dtype=jnp.int32)
    passage_seg = jnp.sum(
        (positions[None, :, None] >= seg_ends[:, None, :]).astype(jnp.int32), axis=2
    )
    question_seg = jnp.zeros((question_count, question_len), jnp.int32)
    question_out, question_kept = encoder_forward(
        question_tokens, question_seg, attn_all[0], inner_all[0], outer_all[0], small_all[0]
    )
    passage_out, passage_kept = encoder_forward(
        passage_tokens, passage_seg, attn_all[1], inner_all[1], outer_all[1], small_all[1]
    )
    question_cls = question_out[:, 0].astype(jnp.bfloat16)
    passage_cls = (
        jnp.take_along_axis(passage_out, seg_starts[:, :, None], axis=1)
        .reshape(-1, model_width)
        .astype(jnp.bfloat16)
    )
    every_cls = lax.all_gather(passage_cls, ("dp", "pair"), axis=0, tiled=True)
    score_scale = model_width ** (-0.5)
    scores = jnp.dot(question_cls, every_cls.T, preferred_element_type=jnp.float32) * score_scale
    top_score = jnp.max(scores, axis=1, keepdims=True)
    raised = jnp.exp(scores - top_score)
    soft_scores = raised / jnp.sum(raised, axis=1, keepdims=True)
    columns = jnp.arange(every_cls.shape[0], dtype=jnp.int32)
    target = (columns[None, :] == positives[:, None]).astype(jnp.float32)
    grad_scores = (soft_scores - target).astype(jnp.bfloat16)
    grad_qcls = jnp.dot(grad_scores, every_cls, preferred_element_type=jnp.float32) * score_scale
    grad_pcls = lax.psum_scatter(
        jnp.dot(grad_scores.T, question_cls, preferred_element_type=jnp.float32) * score_scale,
        ("dp", "pair"),
        scatter_dimension=0,
        tiled=True,
    )
    grad_question_out = jnp.zeros_like(question_out).at[:, 0].set(grad_qcls)
    row_index = jnp.arange(row_count, dtype=jnp.int32)[:, None]
    grad_passage_out = (
        jnp.zeros_like(passage_out)
        .at[row_index, seg_starts]
        .set(grad_pcls.reshape(row_count, -1, model_width))
    )
    question_grad, q_attn, q_inner, q_outer, q_small = encoder_backward(
        question_tokens,
        question_seg,
        attn_all[0],
        inner_all[0],
        outer_all[0],
        small_all[0],
        question_kept,
        grad_question_out,
    )
    passage_grad, p_attn, p_inner, p_outer, p_small = encoder_backward(
        passage_tokens,
        passage_seg,
        attn_all[1],
        inner_all[1],
        outer_all[1],
        small_all[1],
        passage_kept,
        grad_passage_out,
    )
    front_stack = jnp.stack(
        [jnp.concatenate([q_attn, q_inner], axis=1), jnp.concatenate([p_attn, p_inner], axis=1)]
    )
    front_owned = lax.psum_scatter(
        rows_term(front_stack, front_rows * lax.axis_size(("dp", "pair"))),
        ("dp", "pair"),
        scatter_dimension=0,
        tiled=True,
    )
    back_owned = lax.psum_scatter(
        rows_term(jnp.stack([q_outer, p_outer]), back_rows * lax.axis_size(("dp", "pair"))),
        ("dp", "pair"),
        scatter_dimension=0,
        tiled=True,
    )
    small_sum = lax.psum_scatter(
        jnp.stack([q_small, p_small]), ("dp", "pair"), scatter_dimension=1, tiled=True
    )
    front_sum = unfold_rows(front_owned, 2)
    back_sum = unfold_rows(back_owned, 2)
    attn_sum = front_sum[:, :, :attn_cols]
    inner_sum = front_sum[:, :, attn_cols:]
    attn_m, attn_v, attn_w = adam_update(
        attn_weight, attn_first, attn_second, attn_sum, RATE_MATRIX, DECAY_MATRIX
    )
    inner_m, inner_v, inner_w = adam_update(
        ffn_in_weight, ffn_in_first, ffn_in_second, inner_sum, RATE_MATRIX, DECAY_MATRIX
    )
    outer_m, outer_v, outer_w = adam_update(
        ffn_out_weight, ffn_out_first, ffn_out_second, back_sum, RATE_MATRIX, DECAY_MATRIX
    )
    small_m, small_v, small_w = adam_update(
        small_params, small_first, small_second, small_sum, RATE_SMALL, 0.0
    )
    return (
        attn_m,
        attn_v,
        attn_w,
        inner_m,
        inner_v,
        inner_w,
        outer_m,
        outer_v,
        outer_w,
        small_m,
        small_v,
        small_w,
        question_grad,
        passage_grad,
    )


def solution(mesh):
    in_specs = (
        P(("dp", "pair"), None, None),
        P(("dp", "pair"), None, None),
        P(("dp", "pair"), None),
        P(("dp", "pair")),
        P(None, ("dp", "pair"), None),
        P(None, ("dp", "pair"), None),
        P(None, ("dp", "pair"), None),
        P(None, ("dp", "pair"), None),
        P(None, ("dp", "pair"), None),
        P(None, ("dp", "pair"), None),
        P(None, ("dp", "pair"), None),
        P(None, ("dp", "pair"), None),
        P(None, ("dp", "pair"), None),
        P(None, ("dp", "pair")),
        P(None, ("dp", "pair")),
        P(None, ("dp", "pair")),
    )
    out_specs = (
        P(None, ("dp", "pair"), None),
        P(None, ("dp", "pair"), None),
        P(None, ("dp", "pair"), None),
        P(None, ("dp", "pair"), None),
        P(None, ("dp", "pair"), None),
        P(None, ("dp", "pair"), None),
        P(None, ("dp", "pair"), None),
        P(None, ("dp", "pair"), None),
        P(None, ("dp", "pair"), None),
        P(None, ("dp", "pair")),
        P(None, ("dp", "pair")),
        P(None, ("dp", "pair")),
        P(("dp", "pair"), None, None),
        P(("dp", "pair"), None, None),
    )
    return jax.shard_map(local, mesh=mesh, in_specs=in_specs, out_specs=out_specs, check_vma=False)
```

profile of v0, /device:TPU:0, one launch (start us, length us, event | category | flops | bytes accessed | tf_op | source)
XLA Modules:
  0.0 1250.0 jit_solution(14879425951049353167)
XLA Ops:
  14.4 71.1 %all-gather = bf16[32,288,2]{1,2,0:T(2,128)(2,1)S(1)} all-gather(bf16[1,288,2]{1,2,0:T(2,128)(2,1)S(1)} %convert_bitcast_fusion), channel_id=1, replica_groups=mesh['dp'=8,'pair'=4] {'dp','pair'}, dimensions={0}, use_global_device_ids=true | all-gather | bytes 38016 | tf_op jit(solution)/shard_map/all_gather | solution.py:260
  86.6 9.8 all-gather.5.cloned.1.call-done
  96.4 6.9 slice_bitcast_fusion.5
  112.2 5.5 fusion.15
  117.7 4.3 copy.264
  122.0 6.1 reshape.349
  128.1 4.3 reshape.345
  132.4 4.5 fusion.115
  164.7 16.2 %all-gather.7.cloned.1.call-done = bf16[2,768,3072]{2,1,0:T(8,128)(2,1)} async-done(((bf16[2,24,3072]{2,1,0:T(8,128)(2,1)}), bf16[2,768,3072]{2,1,0:T(8,128)(2,1)}) %all-gather.7.cloned.1.call-update) | async-done | bytes 9437200 | tf_op jit(solution)/shard_map/all_gather | solution.py:258
  180.9 20.0 %multiply_convert_fusion.1 = (bf16[512,3072]{1,0:T(8,128)(2,1)}, f32[512,3072]{1,0:T(8,128)}, f32[512,3072]{1,0:T(8,128)}) fusion(f32[3072]{0:T(1024)S(1)} %bitcast.314, bf16[2,768,3072]{2,1,0:T(8,128)(2,1)} %all-gather.7.cloned.1.call-done, f32[512,768]{1,0:T(8,128)S(1)} %get-tuple-element.146, f32[768]{0:T(1024)S(1)} %get-tuple-element.81, ...), kind=kOutput, calls=%fused_computation.17 | convolution fusion | flops 2521694208 | bytes 22042624 | tf_op jit(solution)/shard_map/dot_general | solution.py:89
  200.9 64.3 %all-gather.9.cloned.1.call-done = bf16[2,3072,768]{2,1,0:T(8,128)(2,1)} async-done(((bf16[2,96,768]{2,1,0:T(8,128)(2,1)}), bf16[2,3072,768]{2,1,0:T(8,128)(2,1)}) %all-gather.9.cloned.1.call-update) | async-done | bytes 9437200 | tf_op jit(solution)/shard_map/all_gather | solution.py:259
  265.2 6.0 fusion.122
  274.2 69.5 %all_gather.19 = bf16[256,768]{1,0:T(8,128)(2,1)S(1)} all-gather(bf16[8,768]{1,0:T(8,128)(2,1)S(1)} %select_convert_fusion), channel_id=1, replica_groups=mesh['dp'=8,'pair'=4] {'dp','pair'}, dimensions={0}, use_global_device_ids=true | all-gather | bytes 405504 | tf_op jit(solution)/shard_map/all_gather | solution.py:288
  343.8 20.6 %multiply_convert_fusion.2 = (bf16[512,3072]{1,0:T(8,128)(2,1)S(1)}, f32[512,3072]{1,0:T(8,128)}, f32[512,3072]{1,0:T(8,128)}) fusion(f32[3072]{0:T(1024)S(1)} %bitcast.316, bf16[2,768,3072]{2,1,0:T(8,128)(2,1)} %all-gather.7.cloned.1.call-done, f32[512,768]{1,0:T(8,128)S(1)} %copy-done.25, f32[768]{0:T(1024)S(1)} %get-tuple-element.89, ...), kind=kOutput, calls=%fused_computation.33 | convolution fusion | flops 2521694208 | bytes 22042624 | tf_op jit(solution)/shard_map/dot_general | solution.py:89
  364.4 6.2 fusion.121
  375.3 9.0 convert_reduce_fusion.1
  384.4 4.2 multiply_reduce_fusion.4
  388.7 5.3 convolution_bitcast_fusion.3
  393.9 72.4 %reduce-scatter.9.cloned.1.call-done = f32[8,768]{1,0:T(8,128)} async-done(((f32[256,768]{1,0:T(8,128)}), f32[8,768]{1,0:T(8,128)}) %reduce-scatter.9.cloned.1.call-update) | async-done | bytes 24592 | tf_op jit(solution)/shard_map/reduce_scatter | solution.py:298
  469.5 9.3 convert_reduce_fusion
  488.6 3.9 reshape.407
  492.5 4.1 copy.282
  496.7 3.7 fusion.46
  510.2 4.0 fusion.65
  514.4 4.1 multiply_reduce_fusion
  518.5 5.1 convolution_bitcast_fusion.2
  528.1 3.4 reshape.357
  542.9 6.2 multiply_convert_fusion
  555.1 13.0 %pad_maximum_fusion = f32[2,3072,768]{1,2,0:T(8,128)} fusion(f32[1,3072,768]{1,2,0:T(8,128)} %convolution_bitcast_fusion.2, f32[1,3072,768]{1,2,0:T(8,128)} %convolution_bitcast_fusion.3), kind=kLoop, calls=%fused_computation.5 | loop fusion | flops 4718592 | bytes 37748736 | tf_op jit(solution)/shard_map/stack | solution.py:341
  568.2 18.9 %copy.301 = f32[3072,1536]{1,0:T(8,128)} copy(f32[3072,1536]{0,1:T(8,128)} %bitcast.286) | data formatting | bytes 37748736 | tf_op jit(solution)/shard_map/reshape | solution.py:221
  587.2 9.1 fusion.101
  601.0 3.5 reshape.356
  608.5 4.8 convolution_bitcast_fusion.1
  613.4 8.1 copy.285
  627.8 5.2 convolution_bitcast_fusion
  633.0 5.5 fusion.98
  638.5 5.2 maximum_bitcast_fusion.1
  643.7 13.6 %maximum_bitcast_fusion.2 = f32[1,768,6144]{2,1,0:T(8,128)} fusion(f32[768,3072]{1,0:T(8,128)} %fusion.98, f32[768,768]{1,0:T(8,128)S(1)} %fusion.125, f32[768,2304]{1,0:T(8,128)} %convolution_bitcast_fusion), kind=kLoop, calls=%fused_computation.4 | loop fusion | flops 9437184 | bytes 37748736 | tf_op jit(solution)/shard_map/stack | solution.py:331
  657.3 20.8 %maximum_bitcast_fusion = f32[768,2,6144]{2,0,1:T(8,128)} fusion(f32[1,768,6144]{2,1,0:T(8,128)} %maximum_bitcast_fusion.2, f32[1,768,6144]{2,1,0:T(8,128)S(1)} %maximum_bitcast_fusion.1), kind=kLoop, calls=%fused_computation.2 | loop fusion | flops 9437184 | bytes 75497472 | tf_op jit(solution)/shard_map/transpose | solution.py:221
  678.1 38.6 %copy.298 = f32[768,2,6144]{0,2,1:T(8,128)} copy(f32[768,2,6144]{2,0,1:T(8,128)} %maximum_bitcast_fusion) | data formatting | bytes 75497472 | tf_op jit(solution)/shard_map/transpose | solution.py:221
  716.7 37.2 %copy.321 = f32[768,12288]{1,0:T(8,128)} copy(f32[768,12288]{0,1:T(8,128)} %bitcast.283) | data formatting | bytes 75497472
  755.4 6.3 add_add_fusion.10
  761.7 5.4 add_add_fusion.8
  768.8 105.8 %reduce-scatter.11.cloned.1.call-done = f32[96,1536]{1,0:T(8,128)} async-done(((f32[3072,1536]{1,0:T(8,128)}), f32[96,1536]{1,0:T(8,128)}) %reduce-scatter.11.cloned.1.call-update) | async-done | bytes 589840 | tf_op jit(solution)/shard_map/reduce_scatter | solution.py:340
  877.1 352.8 %reduce-scatter.13.cloned.1.call-done = f32[24,12288]{1,0:T(8,128)} async-done(((f32[768,12288]{1,0:T(8,128)}), f32[24,12288]{1,0:T(8,128)}) %reduce-scatter.13.cloned.1.call-update) | async-done | bytes 1179664
  1229.9 4.9 copy.322
  1234.8 4.5 copy.300
  1239.3 3.6 multiply_subtract_fusion.1
  (368 shorter events, 117.2 us)
Async XLA Ops:
  7.2 5.7 copy-start.72
  7.2 7.2 copy-start.70
  7.2 89.2 %all-gather.5.cloned.1.call-start = ((), (), s32[]{:S(2)}) async-start(), calls=%async_computation.4 | async-start | bytes 9732096 | tf_op jit(solution)/shard_map/all_gather | solution.py:257
  9.1 171.8 %all-gather.7.cloned.1.call-start = ((), (), s32[]{:S(2)}) async-start(), calls=%async_computation.5 | async-start | bytes 9732096 | tf_op jit(solution)/shard_map/all_gather | solution.py:258
  11.0 254.3 %all-gather.9.cloned.1.call-start = ((), (), s32[]{:S(2)}) async-start(), calls=%async_computation.6 | async-start | bytes 9732096 | tf_op jit(solution)/shard_map/all_gather | solution.py:259
  12.9 453.5 %reduce-scatter.9.cloned.1.call-start = ((), (), s32[]{:S(2)}) async-start(), calls=%async_computation.7 | async-start | bytes 811008 | tf_op jit(solution)/shard_map/reduce_scatter | solution.py:298
  86.4 178.9 %copy-start.77 = (f32[768]{0:T(1024)}, f32[768]{0:T(1024)S(1)}, u32[]{:S(2)}) copy-start(f32[768]{0:T(1024)S(1)} %get-tuple-element.81) | copy-start | bytes 9220
  86.6 18.8 %copy-start.54 = (bf16[8,64,768]{2,1,0:T(8,128)(2,1)S(1)}, bf16[8,64,768]{2,1,0:T(8,128)(2,1)}, u32[]{:S(2)}) copy-start(bf16[8,64,768]{2,1,0:T(8,128)(2,1)} %param.18) | copy-start | bytes 2359300
  150.9 8.1 copy-start.42
  164.3 100.9 %copy-start.21 = (f32[512,768]{1,0:T(8,128)}, f32[512,768]{1,0:T(8,128)S(1)}, u32[]{:S(2)}) copy-start(f32[512,768]{1,0:T(8,128)S(1)} %get-tuple-element.146) | copy-start | bytes 4718596
  164.7 36.3 %copy-start.67 = (f32[512]{0:T(512)}, f32[512]{0:T(512)S(1)}, u32[]{:S(2)}) copy-start(f32[512]{0:T(512)S(1)} %multiply_reduce_fusion.10) | copy-start | bytes 6148
  180.9 84.4 %copy-start.79 = (f32[768]{0:T(1024)S(1)}, f32[768]{0:T(1024)}, u32[]{:S(2)}) copy-start(f32[768]{0:T(1024)} %get-tuple-element.80) | copy-start | bytes 9220
  271.3 72.5 %copy-start.25 = (f32[512,768]{1,0:T(8,128)S(1)}, f32[512,768]{1,0:T(8,128)}, u32[]{:S(2)}) copy-start(f32[512,768]{1,0:T(8,128)} %copy-done.24) | copy-start | bytes 4718596
  343.8 20.6 %copy-start.26 = (f32[512,768]{1,0:T(8,128)S(1)}, f32[512,768]{1,0:T(8,128)}, u32[]{:S(2)}) copy-start(f32[512,768]{1,0:T(8,128)} %copy-done.24) | copy-start | bytes 4718596
  364.4 6.2 copy-start.93
  364.4 6.6 copy-start.63
  364.4 6.6 copy-start.69
  373.5 393.7 %reduce-scatter.15.cloned.1.call-start = ((), (), s32[]{:S(2)}) async-start(), calls=%async_computation.10 | async-start | bytes 4866048
  374.5 9.9 slice-start.4
  375.3 9.0 copy-start.27
  375.3 9.0 slice-start.5
  375.3 9.0 slice-start.6
  388.7 77.8 %copy-start.66 = (s32[8]{0:T(128)S(1)}, s32[8]{0:T(128)}, u32[]{:S(2)}) copy-start(s32[8]{0:T(128)} %reshape.376) | copy-start | bytes 100
  468.7 10.2 slice-start.7
  469.5 9.4 copy-start.52
  469.5 9.4 copy-start.22
  469.5 9.4 slice-start.8
  469.5 9.4 slice-start.9
  484.2 8.3 copy-start.73
  488.6 8.1 copy-start.2
  504.2 10.0 slice-start
  525.7 7.2 copy-start.3
  542.9 6.2 copy-start.37
  555.1 319.5 %reduce-scatter.11.cloned.1.call-start = ((), (), s32[]{:S(2)}) async-start(), calls=%async_computation.8 | async-start | bytes 19464192 | tf_op jit(solution)/shard_map/reduce_scatter | solution.py:340
  587.1 642.7 %reduce-scatter.13.cloned.1.call-start = ((), (), s32[]{:S(2)}) async-start(), calls=%async_computation.9 | async-start | bytes 38928384
  587.2 9.2 copy-start.6
  587.2 9.1 copy-start.10
  627.8 10.7 slice-start.2
  632.9 5.5 slice-start.3
  755.4 6.3 copy-start.30
  755.4 6.3 copy-start.62
  755.4 6.3 copy-start.76
  761.7 6.5 copy-start.71
  761.7 6.4 copy-start.82
  761.7 6.5 copy-start.83
  761.7 112.9 %copy-start.50 = (f32[2,96,768]{2,1,0:T(8,128)S(1)}, f32[2,96,768]{2,1,0:T(8,128)}, u32[]{:S(2)}) copy-start(f32[2,96,768]{2,1,0:T(8,128)} %param.28) | copy-start | bytes 1769476
  761.7 112.8 %copy-start.59 = (f32[2,96,768]{2,1,0:T(8,128)S(1)}, f32[2,96,768]{2,1,0:T(8,128)}, u32[]{:S(2)}) copy-start(f32[2,96,768]{2,1,0:T(8,128)} %param.30) | copy-start | bytes 1769476
  761.7 112.8 %copy-start.60 = (f32[2,96,768]{2,1,0:T(8,128)S(1)}, f32[2,96,768]{2,1,0:T(8,128)}, u32[]{:S(2)}) copy-start(f32[2,96,768]{2,1,0:T(8,128)} %param.29) | copy-start | bytes 1769476
  (64 other events, 175.6 us)
Sparse Core Ops, SparseCore 0:
  11.7 84.6 all-gather.4
  100.0 80.7 all-gather.6
  184.5 80.6 all-gather.8
  373.6 92.6 reduce-scatter.8
  555.2 105.9 reduce-scatter.14
  668.6 205.8 reduce-scatter.10
  882.1 347.6 reduce-scatter.12
where the time goes:
time: 1260 us; the launch traced here: 1250 us
  waiting for transfers between devices  621 us (49%)
  local copies, waits for them, and re-layouts  212 us (17%)
  matrix products  173 us (14%)
  blocking collectives  141 us (11%)
  other arithmetic  87 us (7%)
  between operations  16.1 us (1%)
    unnamed x9, waiting for transfers between devices  353 us
    reduce_scatter x1, waiting for transfers between devices, local(): lax.psum_scatter(rows_term(jnp.stack([q_outer, p_outer]), back_rows * lax...  106 us
    reduce_scatter x1, waiting for transfers between devices, local(): lax.psum_scatter(jnp.dot(grad_scores.T, question_cls, preferred_element_t...  72.4 us
    all_gather x1, blocking collectives, local(): lax.all_gather(small_params.astype(jnp.bfloat16), ('dp', 'pair'), axis=1,...  71.1 us
    all_gather x1, blocking collectives, local(): every_cls = lax.all_gather(passage_cls, ('dp', 'pair'), axis=0, tiled=True)  69.5 us
    unnamed x241, local copies, waits for them, and re-layouts  69.3 us
    all_gather x1, waiting for transfers between devices, local(): lax.all_gather(ffn_out_weight.astype(jnp.bfloat16), ('dp', 'pair'), axis=...  64.3 us
    dot_general x2, matrix products, encoder_forward(): jnp.dot(normed_one.astype(jnp.bfloat16), inner_weight, preferred_element_...  40.6 us
  transfers between devices with their start and end apart: 7, of which 6 were waited for; matrix products, arithmetic and copies ran while one was open for 26% of the time, Pallas kernels for 0%

commit v1 on v0

--- a/solution.py
+++ b/solution.py
@@ -1,6 +1,10 @@
+import math
+
 import jax
 import jax.numpy as jnp
 from jax import lax
+from jax.experimental import pallas as pl
+from jax.experimental.pallas import tpu as pltpu
 from jax.sharding import PartitionSpec as P
 
 HD = 64
@@ -380,6 +384,688 @@
     )
 
 
+MESH_ID = pl.DeviceIdType.MESH
+LOW = jnp.bfloat16
+F32 = jnp.float32
+
+
+def dot_nn(a, b):
+    return jnp.dot(a, b, preferred_element_type=F32)
+
+
+def dot_nt(a, b):
+    return lax.dot_general(a, b, (((1,), (1,)), ((), ())), preferred_element_type=F32)
+
+
+def dot_tn(a, b):
+    return lax.dot_general(a, b, (((0,), (0,)), ((), ())), preferred_element_type=F32)
+
+
+def expand_heads(rows):
+    head_of = lax.broadcasted_iota(jnp.int32, rows.shape, 1) // HD
+    heads = rows.shape[1] // HD
+    return jnp.concatenate(
+        [jnp.where(head_of == h, rows, jnp.zeros_like(rows)) for h in range(heads)], axis=0
+    )
+
+
+def pick_heads(stacked):
+    width = stacked.shape[1]
+    heads = width // HD
+    head_of = lax.broadcasted_iota(jnp.int32, (16, width), 1) // HD
+    total = jnp.zeros((16, width), F32)
+    for h in range(heads):
+        total = total + jnp.where(head_of == h, stacked[16 * h : 16 * h + 16], 0.0)
+    return total
+
+
+def split_low(values):
+    high = values.astype(LOW)
+    return high, (values - high.astype(F32)).astype(LOW)
+
+
+def gelu_parts(values):
+    cdf = 0.5 * (1.0 + lax.erf(values * (0.5**0.5)))
+    density = jnp.exp(-0.5 * values * values) * (0.5 / math.pi) ** 0.5
+    return values * cdf, cdf + values * density
+
+
+def step_kernel(
+    qt_ref, pt_ref, attn_ref, ffi_ref, ffo_ref, small_ref, bnd_ref,
+    ga_ref, gi_ref, go_ref, gs_ref, dxq_ref, dxp_ref,
+    X, slabA, slabI, slabO, smb, bndb, R, WN, sn, sno, ST, Pf, Pb, DSb, Emat, b1p,
+    w1s_, w1r, W1, W2, Yb, P2s, P2r, XH, Dout, dZb, Gb, Act, P3s, P3r, Qb, dAb, dUb, dQb,
+    m1s, m1r, m2s, m2r, dws, dwr, sgs, sgr, GS, GSw, GA, GI, GO, DX, qsb, vtb, ybf,
+    loc, sib_s, sib_r, at_s, at_r, ag_s, ag_z, ag_p, aa_s, aa_r, out_l, out_s, out_r,
+):
+    dp, z = lax.axis_index("dp"), lax.axis_index("pair")
+    core = lax.rem(dp, 2)
+    y, x = dp // 4, lax.rem(dp // 2, 2)
+    own = y * 8 + x * 4 + z
+    line = y * 8 + x * 4
+
+    def dev(slot, k):
+        return ((slot // 8) * 4 + lax.rem(slot // 4, 2) * 2 + k, lax.rem(slot, 4))
+
+    sibling = dev(own, 1 - core)
+    slot_x = y * 8 + (1 - x) * 4 + z
+    slot_y = (1 - y) * 8 + x * 4 + z
+    slot_d = (1 - y) * 8 + (1 - x) * 4 + z
+
+    def remote(src, dst, ssem, rsem, target):
+        return pltpu.make_async_remote_copy(
+            src_ref=src, dst_ref=dst, send_sem=ssem, recv_sem=rsem,
+            device_id=target, device_id_type=MESH_ID,
+        )
+
+    def done(ref, sem):
+        pltpu.make_async_copy(ref, ref, sem).wait()
+
+    barrier = pltpu.get_barrier_semaphore()
+
+    def greet(r, c):
+        pl.semaphore_signal(
+            barrier, inc=1, device_id=dev(lax.rem(own + r, 16), core), device_id_type=MESH_ID
+        )
+        return c
+
+    lax.fori_loop(1, 16, greet, 0)
+    pl.semaphore_signal(barrier, inc=1, device_id=sibling, device_id_type=MESH_ID)
+
+    rows = pl.ds(pl.multiple_of(512 * core, 512), 512)
+    pltpu.make_async_copy(attn_ref.at[core], slabA.at[core], loc.at[0]).start()
+    pltpu.make_async_copy(small_ref.at[core], smb.at[own, core], loc.at[1]).start()
+    pltpu.make_async_copy(bnd_ref.at[core], bndb.at[core], loc.at[2]).start()
+
+    @pl.when(core == 0)
+    def _():
+        pltpu.make_async_copy(qt_ref, X.at[rows], loc.at[3]).start()
+
+    @pl.when(core == 1)
+    def _():
+        pltpu.make_async_copy(pt_ref, X.at[rows], loc.at[3]).start()
+
+    pltpu.make_async_copy(ffi_ref.at[core], slabI.at[core], loc.at[4]).start()
+    pltpu.make_async_copy(ffo_ref.at[core], slabO.at[core], loc.at[5]).start()
+    pl.semaphore_wait(barrier, 16)
+
+    other = 1 - core
+    remote(attn_ref.at[other], slabA.at[core], sib_s.at[0], sib_r.at[0], sibling).start()
+    remote(small_ref.at[other], smb.at[own, core], sib_s.at[1], sib_r.at[1], sibling).start()
+    remote(bnd_ref.at[other], bndb.at[core], sib_s.at[2], sib_r.at[2], sibling).start()
+
+    @pl.when(core == 0)
+    def _():
+        remote(pt_ref, X.at[rows], sib_s.at[3], sib_r.at[3], sibling).start()
+
+    @pl.when(core == 1)
+    def _():
+        remote(qt_ref, X.at[rows], sib_s.at[3], sib_r.at[3], sibling).start()
+
+    remote(ffi_ref.at[other], slabI.at[core], sib_s.at[4], sib_r.at[4], sibling).start()
+    remote(ffo_ref.at[other], slabO.at[core], sib_s.at[5], sib_r.at[5], sibling).start()
+
+    done(slabA.at[core], loc.at[0])
+    done(slabA.at[other], sib_r.at[0])
+    for m in range(4):
+        cols = slice(768 * m, 768 * m + 768)
+        R[own, m] = jnp.concatenate([slabA[0, :, cols], slabA[1, :, cols]], axis=0).astype(LOW)
+        for target in (slot_x, slot_y):
+            remote(R.at[own, m], R.at[own, m], at_s.at[m], at_r.at[own, m, 0], dev(target, core)).start()
+
+        def along_z(r, c):
+            target = line + lax.rem(z + r, 4)
+            remote(R.at[own, m], R.at[own, m], at_s.at[m], at_r.at[own, m, 0], dev(target, core)).start()
+            return c
+
+        lax.fori_loop(1, 4, along_z, 0)
+
+    done(smb.at[own, core], loc.at[1])
+    done(smb.at[own, other], sib_r.at[1])
+
+    def direct(src_of, dst, ssem, rsem):
+        def body(r, c):
+            target = lax.rem(own + r, 16)
+            remote(src_of(target), dst.at[own], ssem, rsem, dev(target, core)).start()
+            return c
+
+        lax.fori_loop(1, 16, body, 0)
+
+    def direct_done(dst, rsem):
+        done(dst.at[pl.ds(0, 15)], rsem)
+
+    direct(lambda t: smb.at[own], smb, aa_s.at[0], aa_r.at[0])
+
+    def relay(m):
+        def from_z(r, c):
+            slot = line + lax.rem(z + r, 4)
+            done(R.at[slot, m], at_r.at[slot, m, 0])
+            for target in (slot_x, slot_y):
+                remote(R.at[slot, m], R.at[slot, m], at_s.at[m], at_r.at[slot, m, 0], dev(target, core)).start()
+            return c
+
+        lax.fori_loop(1, 4, from_z, 0)
+
+        def from_plane(r, c):
+            zz = lax.rem(z + r, 4)
+            for base, target, half in (
+                (y * 8 + (1 - x) * 4, slot_y, 0),
+                ((1 - y) * 8 + x * 4, slot_x, 1),
+            ):
+                slot = base + zz
+                done(R.at[slot, m], at_r.at[slot, m, 0])
+                part = R.at[slot, m, :, pl.ds(384 * half, 384)]
+                remote(part, part, at_s.at[m], at_r.at[slot, m, half], dev(target, core)).start()
+            return c
+
+        lax.fori_loop(0, 4, from_plane, 0)
+
+    def from_slots(read, write):
+        def body(g, c):
+            got = [read(4 * g + i).astype(F32) for i in range(4)]
+            natural = jnp.concatenate([v[0:24] for v in got] + [v[24:48] for v in got], axis=0)
+            write(pl.ds(pl.multiple_of(192 * g, 64), 192), natural.astype(LOW))
+            return c
+
+        lax.fori_loop(0, 4, body, 0)
+
+    def to_slots(read, write):
+        def body(g, c):
+            v = read(pl.ds(pl.multiple_of(192 * g, 64), 192))
+            for i in range(4):
+                part = jnp.concatenate(
+                    [v[24 * i : 24 * i + 24], v[96 + 24 * i : 96 + 24 * i + 24]], axis=0
+                )
+                write(4 * g + i, part.astype(LOW))
+            return c
+
+        lax.fori_loop(0, 4, body, 0)
+
+    def arrive(m):
+        def body(zz, c):
+            slot = (1 - y) * 8 + (1 - x) * 4 + zz
+            for half in range(2):
+                done(R.at[slot, m, :, pl.ds(384 * half, 384)], at_r.at[slot, m, half])
+            return c
+
+        lax.fori_loop(0, 4, body, 0)
+
+        def write(where, v):
+            WN[m, where, :] = v
+
+        from_slots(lambda s: R[s, m], write)
+
+    def gather_start(buf, n):
+        def body(r, c):
+            target = line + lax.rem(z + r, 4)
+            remote(buf.at[own], buf.at[own], ag_s.at[n], ag_z.at[n], dev(target, core)).start()
+            return c
+
+        lax.fori_loop(1, 4, body, 0)
+
+    def gather_forward(buf, n):
+        done(buf.at[pl.ds(0, 3)], ag_z.at[n])
+        block = buf.at[pl.ds(line, 4)]
+        for target in (slot_x, slot_y, slot_d):
+            remote(block, block, ag_s.at[n], ag_p.at[n], dev(target, core)).start()
+
+    def gather_done(buf, n):
+        done(buf.at[pl.ds(0, 12)], ag_p.at[n])
+
+    def prepare_ffn():
+        row = lax.broadcasted_iota(jnp.int32, (384, 512), 0)
+        col = lax.broadcasted_iota(jnp.int32, (384, 512), 1)
+        Emat[...] = jnp.where(col == 128 * (row // 96) + lax.rem(row, 96), 1.0, 0.0).astype(LOW)
+        done(slabI.at[core], loc.at[4])
+        done(slabI.at[other], sib_r.at[4])
+        for g in range(8):
+            cols = slice(384 * g, 384 * g + 384)
+            part = jnp.concatenate([slabI[0, :, cols], slabI[1, :, cols]], axis=0).astype(LOW)
+            wide = dot_nn(part, Emat[...]).astype(LOW)
+            for i in range(4):
+                w1s_[4 * (g // 2) + i, :, 128 * (g % 2) : 128 * (g % 2) + 128] = wide[
+                    :, 128 * i : 128 * i + 128
+                ]
+        direct(lambda t: w1s_.at[t], w1r, aa_s.at[1], aa_r.at[1])
+        w1r[own] = w1s_[own]
+        done(slabO.at[core], loc.at[5])
+        done(slabO.at[other], sib_r.at[5])
+        gap = jnp.zeros((32, 768), F32)
+        W2[...] = jnp.concatenate([slabO[0], gap, slabO[1], gap], axis=0).astype(LOW)
+
+    def natural_small():
+        direct_done(smb, aa_r.at[0])
+        for g in range(8):
+            parts = [smb[4 * (g // 2) + i, g % 2] for i in range(4)]
+            lines = [parts[0][0:1], parts[0][1:2]]
+            for i in range(1, 4):
+                lines += [parts[i - 1][2:3] + parts[i][0:1], parts[i][1:2]]
+            lines += [parts[3][2:3]]
+            sn[9 * g : 9 * g + 9, :] = jnp.concatenate(lines, axis=0)
+        remote(sn, sno, sib_s.at[6], sib_r.at[6], sibling).start()
+
+    def vec(row, count=6, ref=sn):
+        return jnp.concatenate([ref[row + i : row + i + 1, :] for i in range(count)], axis=1)
+
+    relay(0)
+    done(bndb.at[core], loc.at[2])
+    done(bndb.at[other], sib_r.at[2])
+    done(X.at[pl.ds(0, 512)], loc.at[3])
+    done(X.at[pl.ds(0, 512)], sib_r.at[3])
+    starts = jnp.concatenate([bndb[0, 0:8], bndb[1, 0:8] + 512], axis=0)[:, 0:1]
+    ends = jnp.concatenate([bndb[0, 8:16], bndb[1, 8:16] + 512], axis=0)[:, 0:1]
+    token = lax.broadcasted_iota(jnp.int32, (16, 1024), 1)
+    inside = jnp.logical_and(token >= starts, token < ends)
+    first = jnp.where(token == starts, 1.0, 0.0).astype(LOW)
+    cls_in = dot_nn(first, X[...])
+    cls_low = cls_in.astype(LOW)
+    natural_small()
+    relay(1)
+    arrive(0)
+    queries = (dot_nn(cls_low, WN[0]) + vec(0)).astype(LOW)
+    Qb[own] = queries
+    relay(2)
+    arrive(1)
+    qsb[...] = (dot_nt(expand_heads(queries), WN[1]) * (HD**-0.5)).astype(LOW)
+    ST[...] = dot_nt(qsb[...], X[...])
+
+    def soften(h, c):
+        at = pl.ds(pl.multiple_of(16 * h, 16), 16)
+        s = jnp.where(inside, ST[at, :], -1000000000.0)
+        e = jnp.exp(s - jnp.max(s, axis=1, keepdims=True))
+        p = e / jnp.sum(e, axis=1, keepdims=True)
+        Pf[at, :] = p
+        Pb[at, :] = p.astype(LOW)
+        return c
+
+    lax.fori_loop(0, 12, soften, 0)
+    relay(3)
+    ybf[...] = dot_nn(Pb[...], X[...]).astype(LOW)
+    prepare_ffn()
+    arrive(2)
+    mixed = (pick_heads(dot_nn(ybf[...], WN[2])) + vec(6)).astype(LOW)
+    arrive(3)
+    lifted = cls_in + dot_nn(mixed, WN[3]) + vec(12)
+    centred = lifted - jnp.mean(lifted, axis=1, keepdims=True)
+    rstd_one = lax.rsqrt(jnp.mean(centred * centred, axis=1, keepdims=True) + NORM_EPS)
+    hat_one = centred * rstd_one
+    normed = hat_one * vec(18) + vec(24)
+    Yb[own] = normed.astype(LOW)
+    gather_start(Yb, 0)
+    gather_start(Qb, 1)
+
+    early = jnp.concatenate(
+        [ybf[...].astype(F32), cls_in, mixed.astype(F32), jnp.zeros((32, 768), F32)], axis=0
+    )
+    DX[0:768, 0:256] = early.T
+
+    def write_m1(slot, v):
+        m1s[slot] = v
+
+    to_slots(lambda w: DX[w, 0:256], write_m1)
+    m1r[own] = m1s[own]
+    gather_forward(Yb, 0)
+
+    b1 = jnp.concatenate([vec(30 + 3 * g, 3) for g in range(8)], axis=0).astype(LOW)
+    b1_wide = dot_nn(b1, Emat[...])
+    for g in range(8):
+        b1p[g] = jnp.broadcast_to(b1_wide[g : g + 1], (8, 512))
+    group = pl.multiple_of(128 * z, 128)
+    gy = 4 * y + 2 * x
+    b1_row = jnp.concatenate(
+        [b1p[gy, 0:1, pl.ds(group, 128)], b1p[gy + 1, 0:1, pl.ds(group, 128)]], axis=1
+    )
+    direct_done(w1r, aa_r.at[1])
+
+    def write_w1(where, v):
+        W1[where, :] = v
+
+    from_slots(lambda s: w1r[s], write_w1)
+    gather_done(Yb, 0)
+    all_y = Yb[...].reshape(256, 768)
+    act = dot_nn(all_y, W1[...]) + b1_row
+    Act[...] = act
+    hidden, unused = gelu_parts(act)
+    Gb[...] = hidden.astype(LOW)
+    P2s[...] = dot_nn(Gb[...], W2[...]).astype(LOW).reshape(16, 16, 768)
+    direct(lambda t: P2s.at[t], P2r, aa_s.at[2], aa_r.at[2])
+    P2r[own] = P2s[own]
+    gather_forward(Qb, 1)
+    direct_done(P2r, aa_r.at[2])
+    direct(lambda t: m1s.at[t], m1r, aa_s.at[3], aa_r.at[3])
+    second = normed + jnp.sum(P2r[...].astype(F32), axis=0) + vec(54)
+    centred = second - jnp.mean(second, axis=1, keepdims=True)
+    rstd_two = lax.rsqrt(jnp.mean(centred * centred, axis=1, keepdims=True) + NORM_EPS)
+    hat_two = centred * rstd_two
+    rstd_high, rstd_low = split_low(rstd_two)
+    lane = lax.broadcasted_iota(jnp.int32, (16, 128), 1)
+    positive = jnp.concatenate([bndb[0, 16:24], bndb[1, 16:24]], axis=0).astype(F32)
+    extra = jnp.where(
+        lane == 0, rstd_high.astype(F32),
+        jnp.where(lane == 1, rstd_low.astype(F32), jnp.where(lane == 2, positive, 0.0)),
+    )
+    XH[core, own] = jnp.concatenate([hat_two, extra], axis=1).astype(LOW)
+    mine = XH.at[core]
+    gather_start(mine, 2)
+    gather_forward(mine, 2)
+    gather_done(mine, 2)
+    remote(XH.at[core], XH.at[core], sib_s.at[7], sib_r.at[7], sibling).start()
+    done(sno, sib_r.at[6])
+    done(XH.at[other], sib_r.at[7])
+
+    def vec_of(encoder, row):
+        return jnp.where(core == encoder, vec(row), vec(row, 6, sno))
+
+    xq = XH[0].reshape(256, 896).astype(F32)
+    xp = XH[1].reshape(256, 896).astype(F32)
+    qc = (xq[:, 0:768] * vec_of(0, 60) + vec_of(0, 66)).astype(LOW)
+    pc = (xp[:, 0:768] * vec_of(1, 60) + vec_of(1, 66)).astype(LOW)
+    scale = 768 ** (-0.5)
+    scores = dot_nt(qc, pc) * scale
+    raised = jnp.exp(scores - jnp.max(scores, axis=1, keepdims=True))
+    soft = raised / jnp.sum(raised, axis=1, keepdims=True)
+    place = lax.broadcasted_iota(jnp.int32, (256, 256), 1)
+    slot_of = place // 16
+    owner_of = (
+        16 * (slot_of // 8) + 8 * lax.rem(slot_of // 4, 2)
+        + 4 * (lax.rem(place, 16) // 8) + lax.rem(slot_of, 4)
+    )
+    passage = (8 * owner_of + lax.rem(place, 8)).astype(F32)
+    target = jnp.where(passage == xq[:, 770:771], 1.0, 0.0)
+    grad_scores = (soft - target).astype(LOW)
+
+    @pl.when(core == 0)
+    def _():
+        Dout[...] = dot_nn(grad_scores, pc) * scale
+
+    @pl.when(core == 1)
+    def _():
+        Dout[...] = dot_tn(grad_scores, qc) * scale
+
+    dout = Dout[...]
+    block = XH[core].reshape(256, 896).astype(F32)
+    hat = block[:, 0:768]
+    rstd = block[:, 768:769] + block[:, 769:770]
+    inner = dout * vec(60)
+    grad_two = rstd * (
+        inner - jnp.mean(inner, axis=1, keepdims=True)
+        - hat * jnp.mean(inner * hat, axis=1, keepdims=True)
+    )
+    dg2 = jnp.sum(dout * hat, axis=0, keepdims=True)
+    ds2 = jnp.sum(dout, axis=0, keepdims=True)
+    Dout[...] = grad_two
+    dZb[...] = grad_two.astype(LOW)
+    db2 = jnp.sum(dZb[...].astype(F32), axis=0, keepdims=True)
+    unused, slope = gelu_parts(Act[...])
+    da = (dot_nt(dZb[...], W2[...]) * slope).astype(LOW)
+    P3s[...] = dot_nt(da, W1[...]).astype(LOW).reshape(16, 16, 768)
+    direct(lambda t: P3s.at[t], P3r, aa_s.at[4], aa_r.at[4])
+    P3r[own] = P3s[own]
+    db1 = jnp.sum(da.astype(F32), axis=0, keepdims=True)
+    dw2 = dot_tn(Gb[...], dZb[...])
+    GO[0] = dw2[0:96]
+    GO[1] = dw2[128:224]
+    pltpu.make_async_copy(GO.at[core], go_ref.at[core], out_l.at[0]).start()
+    remote(GO.at[other], go_ref.at[core], out_s.at[0], out_r.at[0], sibling).start()
+    DX[0:768, 0:256] = dot_tn(all_y, da)
+
+    def write_dw(slot, v):
+        dws[slot] = v
+
+    to_slots(lambda w: DX[w, 0:256], write_dw)
+    dwr[own] = dws[own]
+    own_rows = pl.ds(pl.multiple_of(16 * own, 16), 16)
+    direct_done(P3r, aa_r.at[4])
+
+    grad_normed = Dout[own_rows, :] + jnp.sum(P3r[...].astype(F32), axis=0)
+    inner = grad_normed * vec(18)
+    grad_one = rstd_one * (
+        inner - jnp.mean(inner, axis=1, keepdims=True)
+        - hat_one * jnp.mean(inner * hat_one, axis=1, keepdims=True)
+    )
+    grad_lift = grad_one.astype(LOW)
+    grad_mixed = dot_nt(grad_lift, WN[3]).astype(LOW)
+    dUb[own] = grad_lift
+    dAb[own] = grad_mixed
+    gather_start(dUb, 3)
+    gather_start(dAb, 4)
+    direct(lambda t: dws.at[t], dwr, aa_s.at[5], aa_r.at[5])
+    dg1 = jnp.sum(grad_normed * hat_one, axis=0, keepdims=True)
+    ds1 = jnp.sum(grad_normed, axis=0, keepdims=True)
+    sgs[...] = jnp.concatenate(
+        [dg1[:, 128 * i : 128 * i + 128] for i in range(6)]
+        + [ds1[:, 128 * i : 128 * i + 128] for i in range(6)]
+        + [db1[:, 0:128], db1[:, 128:256], jnp.zeros((2, 128), F32)], axis=0,
+    )
+    direct(lambda t: sgs, sgr, aa_s.at[6], aa_r.at[6])
+    sgr[own] = sgs[...]
+    spread = expand_heads(grad_mixed)
+    vtb[...] = dot_nt(spread, WN[2]).astype(LOW)
+    constant = jnp.sum(spread.astype(F32) * vec(6), axis=1, keepdims=True)
+    ST[...] = dot_nt(vtb[...], X[...]) + constant
+
+    def harden(h, c):
+        at = pl.ds(pl.multiple_of(16 * h, 16), 16)
+        p, dprob = Pf[at, :], ST[at, :]
+        total = jnp.sum(p * dprob, axis=1, keepdims=True)
+        DSb[at, :] = (p * (dprob - total)).astype(LOW)
+        return c
+
+    lax.fori_loop(0, 12, harden, 0)
+    late = (dot_nn(DSb[...], X[...]) * (HD**-0.5)).astype(LOW)
+    DX[0:768, 0:256] = jnp.concatenate(
+        [late.astype(F32), jnp.zeros((64, 768), F32)], axis=0
+    ).T
+
+    def write_m2(slot, v):
+        m2s[slot] = v
+
+    to_slots(lambda w: DX[w, 0:256], write_m2)
+    direct(lambda t: m2s.at[t], m2r, aa_s.at[7], aa_r.at[7])
+    m2r[own] = m2s[own]
+    grad_query = pick_heads(dot_nn(late, WN[1])).astype(LOW)
+    dQb[own] = grad_query
+    gather_start(dQb, 5)
+    gather_forward(dUb, 3)
+    gather_forward(dAb, 4)
+    gather_forward(dQb, 5)
+
+    grad_cls = grad_one + dot_nt(grad_query, WN[0])
+    cls_high, cls_rest = split_low(grad_cls)
+    right = jnp.concatenate([qsb[...], vtb[...], cls_high, cls_rest], axis=0)
+    for k in range(2):
+        part = slice(512 * k, 512 * k + 512)
+        left = jnp.concatenate([DSb[:, part], Pb[:, part], first[:, part], first[:, part]], axis=0)
+        DX[part, :] = dot_tn(left, right)
+    other_rows = pl.ds(pl.multiple_of(512 * other, 512), 512)
+
+    @pl.when(core == 0)
+    def _():
+        pltpu.make_async_copy(DX.at[rows], dxq_ref, out_l.at[1]).start()
+        remote(DX.at[other_rows], dxq_ref, out_s.at[1], out_r.at[1], sibling).start()
+
+    @pl.when(core == 1)
+    def _():
+        pltpu.make_async_copy(DX.at[rows], dxp_ref, out_l.at[1]).start()
+        remote(DX.at[other_rows], dxp_ref, out_s.at[1], out_r.at[1], sibling).start()
+
+    direct_done(dwr, aa_r.at[5])
+    for g in range(8):
+        wide = jnp.concatenate(
+            [dwr[4 * (g // 2) + i, :, 128 * (g % 2) : 128 * (g % 2) + 128] for i in range(4)], axis=1
+        )
+        narrow = dot_nt(wide, Emat[...])
+        GI[0, :, 384 * g : 384 * g + 384] = narrow[0:24]
+        GI[1, :, 384 * g : 384 * g + 384] = narrow[24:48]
+    pltpu.make_async_copy(GI.at[core], gi_ref.at[core], out_l.at[2]).start()
+    remote(GI.at[other], gi_ref.at[core], out_s.at[2], out_r.at[2], sibling).start()
+
+    def put(m, v):
+        GA[0, :, 768 * m : 768 * m + 768] = v[0:24]
+        GA[1, :, 768 * m : 768 * m + 768] = v[24:48]
+
+    def factor_sum(messages, columns):
+        def body(s, total):
+            wide = jnp.concatenate(
+                [expand_heads(columns[s]), jnp.zeros((64, 768), LOW)], axis=0
+            )
+            return total + dot_nn(messages[s], wide)
+
+        return lax.fori_loop(0, 16, body, jnp.zeros((48, 768), F32))
+
+    gather_done(Qb, 1)
+    gather_done(dAb, 4)
+    direct_done(m1r, aa_r.at[3])
+    put(2, factor_sum(m1r, dAb))
+    gather_done(dUb, 3)
+
+    def columns_of(at):
+        return jnp.concatenate(
+            [m1r[s, :, at : at + 16].astype(F32) for s in range(16)], axis=1
+        ).astype(LOW)
+
+    all_du = dUb[...].reshape(256, 768)
+    put(3, dot_nn(columns_of(208), all_du))
+    direct_done(m2r, aa_r.at[7])
+    put(1, factor_sum(m2r, Qb))
+    gather_done(dQb, 5)
+    all_dq = dQb[...].reshape(256, 768)
+    put(0, dot_nn(columns_of(192), all_dq))
+    pltpu.make_async_copy(GA.at[core], ga_ref.at[core], out_l.at[3]).start()
+    remote(GA.at[other], ga_ref.at[core], out_s.at[3], out_r.at[3], sibling).start()
+
+    direct_done(sgr, aa_r.at[6])
+    sums = jnp.sum(sgr[...], axis=0)
+    hidden_rows = []
+    for g in range(8):
+        wide = jnp.concatenate(
+            [sgr[4 * (g // 2) + i, 12 + g % 2 : 13 + g % 2, :] for i in range(4)], axis=1
+        )
+        hidden_rows.append(wide)
+    wide = jnp.concatenate(hidden_rows, axis=0)
+    high, rest = split_low(wide)
+    rest, last = split_low(wide - high.astype(F32))
+    narrow = dot_nt(high, Emat[...]) + dot_nt(rest, Emat[...]) + dot_nt(last, Emat[...])
+
+    def six(v):
+        return [v[:, 128 * i : 128 * i + 128] for i in range(6)]
+
+    lines = six(jnp.sum(all_dq.astype(F32), axis=0, keepdims=True))
+    lines += six(jnp.sum(dAb[...].reshape(256, 768).astype(F32), axis=0, keepdims=True))
+    lines += six(jnp.sum(all_du.astype(F32), axis=0, keepdims=True))
+    lines += [sums[0:12]]
+    for g in range(8):
+        lines += [narrow[g : g + 1, 128 * i : 128 * i + 128] for i in range(3)]
+    lines += six(db2) + six(dg2) + six(ds2) + [jnp.zeros((8, 128), F32)]
+    packed = jnp.concatenate(lines, axis=0)
+    for g in range(8):
+        for i in range(4):
+            at = 9 * g + 9 * i // 4
+            GS[g, i] = packed[at : at + 8]
+    for k in range(2):
+        GSw[k] = GS[gy + k, z]
+    pltpu.make_async_copy(GSw.at[core], gs_ref.at[core], out_l.at[4]).start()
+    remote(GSw.at[other], gs_ref.at[core], out_s.at[4], out_r.at[4], sibling).start()
+
+    for n, (mine_ref, theirs) in enumerate(
+        ((GO.at[0], GO.at[0]), (DX.at[rows], DX.at[rows]), (GI.at[0], GI.at[0]),
+         (GA.at[0], GA.at[0]), (GSw.at[0], GSw.at[0]))
+    ):
+        done(mine_ref, out_l.at[n])
+        done(theirs, out_s.at[n])
+        done(theirs, out_r.at[n])
+    for n, ref in enumerate(
+        (slabA.at[0], smb.at[0, 0], bndb.at[0], X.at[rows], slabI.at[0], slabO.at[0], sn, XH.at[0])
+    ):
+        done(ref, sib_s.at[n])
+    for m in range(4):
+        done(R.at[pl.ds(0, 15), m], at_s.at[m])
+    for n, ref in enumerate((Yb, Qb, XH.at[0], dUb, dAb, dQb)):
+        done(ref.at[pl.ds(0, 15)], ag_s.at[n])
+    for n, ref in enumerate((smb, w1r, P2r, m1r, P3r, dwr, sgr, m2r)):
+        done(ref.at[pl.ds(0, 15)], aa_s.at[n])
+
+
+def kernel_call(qt, pt, attn, ffi, ffo, small, bnd):
+    any_space = pl.BlockSpec(memory_space=pl.ANY)
+    vmem = pl.BlockSpec(memory_space=pltpu.VMEM)
+    V = pltpu.VMEM
+    dma = pltpu.SemaphoreType.DMA
+    scratch = [
+        V((1024, 768), LOW), V((2, 24, 3072), F32), V((2, 24, 3072), F32), V((2, 96, 768), F32),
+        V((16, 2, 8, 128), F32), V((2, 24, 128), jnp.int32), V((16, 4, 48, 768), LOW),
+        V((4, 768, 768), LOW), V((72, 128), F32), V((72, 128), F32), V((192, 1024), F32),
+        V((192, 1024), F32), V((192, 1024), LOW), V((192, 1024), LOW), V((384, 512), LOW),
+        V((8, 8, 512), F32),
+        V((16, 48, 256), LOW), V((16, 48, 256), LOW), V((768, 256), LOW), V((256, 768), LOW),
+        V((16, 16, 768), LOW), V((16, 16, 768), LOW), V((16, 16, 768), LOW),
+        V((2, 16, 16, 896), LOW), V((256, 768), F32), V((256, 768), LOW), V((256, 256), LOW),
+        V((256, 256), F32), V((16, 16, 768), LOW), V((16, 16, 768), LOW), V((16, 16, 768), LOW),
+        V((16, 16, 768), LOW), V((16, 16, 768), LOW), V((16, 16, 768), LOW),
+        V((16, 48, 256), LOW), V((16, 48, 256), LOW), V((16, 48, 256), LOW), V((16, 48, 256), LOW),
+        V((16, 48, 256), LOW), V((16, 48, 256), LOW), V((16, 128), F32), V((16, 16, 128), F32),
+        V((8, 4, 8, 128), F32), V((2, 8, 128), F32), V((2, 24, 3072), F32), V((2, 24, 3072), F32),
+        V((2, 96, 768), F32), V((1024, 768), F32), V((192, 768), LOW), V((192, 768), LOW),
+        V((192, 768), LOW),
+        dma((6,)), dma((8,)), dma((8,)), dma((4,)), dma((16, 4, 2)), dma((6,)), dma((6,)),
+        dma((6,)), dma((8,)), dma((8,)), dma((5,)), dma((5,)), dma((5,)),
+    ]
+    shapes = (
+        (2, 24, 3072), (2, 24, 3072), (2, 96, 768), (2, 8, 128), (512, 768), (512, 768)
+    )
+    return pl.pallas_call(
+        step_kernel,
+        out_shape=[jax.ShapeDtypeStruct(s, F32) for s in shapes],
+        in_specs=[any_space] * 5 + [vmem] * 2,
+        out_specs=[any_space] * 6,
+        scratch_shapes=scratch,
+        compiler_params=pltpu.CompilerParams(
+            collective_id=0, has_side_effects=True, vmem_limit_bytes=56 << 20
+        ),
+    )(qt, pt, attn, ffi, ffo, small, bnd)
+
+
+def local_kernel(
+    question_tokens, passage_tokens, passage_lengths, positives,
+    attn_weight, attn_first, attn_second, ffn_in_weight, ffn_in_first, ffn_in_second,
+    ffn_out_weight, ffn_out_first, ffn_out_second, small_params, small_first, small_second,
+):
+    pair = lax.axis_index("pair")
+    zero = jnp.zeros((), jnp.int32)
+    low_small = small_params.astype(LOW).astype(F32)
+    window = lax.dynamic_update_slice(jnp.zeros((2, 1024), F32), low_small, (zero, 32 * pair))
+    ends = jnp.cumsum(passage_lengths, axis=1)
+    base = jnp.array([[0], [256]], jnp.int32)
+    passage_ends = (ends + base).reshape(8)
+    passage_starts = (ends - passage_lengths + base).reshape(8)
+    question_starts = jnp.arange(8, dtype=jnp.int32) * 64
+    marks = jnp.stack(
+        [
+            jnp.concatenate([question_starts, question_starts + 64, positives]),
+            jnp.concatenate([passage_starts, passage_ends, positives]),
+        ]
+    )
+    bounds = jnp.broadcast_to(marks[:, :, None], (2, 24, 128))
+    grads = kernel_call(
+        question_tokens.reshape(512, 768), passage_tokens.reshape(512, 768),
+        attn_weight, ffn_in_weight, ffn_out_weight, window.reshape(2, 8, 128), bounds,
+    )
+    attn_sum, inner_sum, outer_sum, small_window, grad_question, grad_passage = grads
+    small_sum = lax.dynamic_slice(small_window.reshape(2, 1024), (zero, 32 * pair), (2, 288))
+    return (
+        *adam_update(attn_weight, attn_first, attn_second, attn_sum, RATE_MATRIX, DECAY_MATRIX),
+        *adam_update(ffn_in_weight, ffn_in_first, ffn_in_second, inner_sum, RATE_MATRIX, DECAY_MATRIX),
+        *adam_update(ffn_out_weight, ffn_out_first, ffn_out_second, outer_sum, RATE_MATRIX, DECAY_MATRIX),
+        *adam_update(small_params, small_first, small_second, small_sum, RATE_SMALL, 0.0),
+        grad_question.reshape(question_tokens.shape),
+        grad_passage.reshape(passage_tokens.shape),
+    )
+
+
+def fits_kernel(mesh):
+    return mesh.shape["dp"] == 8 and mesh.shape["pair"] == 4
+
+
 def solution(mesh):
     in_specs = (
         P(("dp", "pair"), None, None),
@@ -415,4 +1101,5 @@
         P(("dp", "pair"), None, None),
         P(("dp", "pair"), None, None),
     )
-    return jax.shard_map(local, mesh=mesh, in_specs=in_specs, out_specs=out_specs, check_vma=False)
+    body = local_kernel if fits_kernel(mesh) else local
+    return jax.shard_map(body, mesh=mesh, in_specs=in_specs, out_specs=out_specs, check_vma=False)

time: 1260 us -> 179 us (0.14)
  waiting for transfers between devices: 621 us -> 0 us
  local copies, waits for them, and re-layouts: 212 us -> 6.67 us
  matrix products: 173 us -> 0 us
  Pallas kernels: 0 us -> 161 us
  blocking collectives: 141 us -> 0 us
  other arithmetic: 87 us -> 9.41 us
  between operations: 16.1 us -> 0.8 us
    unnamed x9 -> x0, waiting for transfers between devices: 353 us -> none
    reduce_scatter x2 -> x0, waiting for transfers between devices: 178 us -> none  [the longest x1 106 us: local(): lax.psum_scatter(rows_term(jnp.stack([q_outer, p_outer]), back_rows * lax...]
    dot_general x39 -> x0, matrix products: 173 us -> none  [the longest x2 40.6 us: encoder_forward(): jnp.dot(normed_one.astype(jnp.bfloat16), inner_weight, preferred_element_...]
    pallas_call x0 -> x1, Pallas kernels: none -> 161 us  [kernel_call(): pl.pallas_call(step_kernel, out_shape=[jax.ShapeDtypeStruct(s, F32) for s...]
    all_gather x2 -> x0, blocking collectives: 141 us -> none  [the longest x1 71.1 us: local(): lax.all_gather(small_params.astype(jnp.bfloat16), ('dp', 'pair'), axis=1,...]
    all_gather x3 -> x0, waiting for transfers between devices: 90.3 us -> none  [the longest x1 64.3 us: local(): lax.all_gather(ffn_out_weight.astype(jnp.bfloat16), ('dp', 'pair'), axis=...]
    unnamed x241 -> x36, local copies, waits for them, and re-layouts: 69.3 us -> 5.74 us
    reshape x11 -> x1, local copies, waits for them, and re-layouts: 55.5 us -> 0.08 us  [local_kernel(): passage_starts = (ends - passage_lengths + base).reshape(8)]
  transfers between devices with their start and end apart: 7 -> 0, of which waited for: 6 -> 0; matrix products, arithmetic and copies ran while one was open for 26% -> 0% of each run, Pallas kernels for 0% -> 0%
where the time goes in v1:
time: 179 us; the launch traced here: 178 us
  Pallas kernels  161 us (90%)
  other arithmetic  9.41 us (5%)
  local copies, waits for them, and re-layouts  6.67 us (4%)
    pallas_call x1, Pallas kernels, kernel_call(): pl.pallas_call(step_kernel, out_shape=[jax.ShapeDtypeStruct(s, F32) for s...  161 us
    sub x4, other arithmetic, adam_update(): weight - step_rate * (update + decay_rate * weight)  6.37 us
    unnamed x36, local copies, waits for them, and re-layouts  5.74 us

profile of v1, /device:TPU:0, one launch (start us, length us, event | category | flops | bytes accessed | tf_op | source)
XLA Modules:
  0.0 178.3 jit_solution(676543154147617469)
XLA Ops:
  0.7 0.9 reduce_window_sum.11
  1.5 0.7 subtract_add_fusion
  2.3 0.1 reshape.57
  2.3 0.1 add.87
  2.4 0.7 add_bitcast_fusion
  3.2 0.7 convert_convert_fusion
  3.9 0.1 dynamic_update_slice.3
  4.0 0.6 copy.36
  4.6 0.7 broadcast_in_dim.10.bnd_ref
  5.2 0.0 copy-start.14
  5.2 0.0 copy-start.15
  5.2 0.0 copy-start
  5.3 0.0 copy-start.5
  5.3 0.0 copy-start.6
  5.3 161.5 %shard_map.272 = (f32[2,24,3072]{2,1,0:T(8,128)}, f32[2,24,3072]{2,1,0:T(8,128)}, f32[2,96,768]{2,1,0:T(8,128)}, f32[2,8,128]{2,1,0:T(8,128)}, f32[512,768]{1,0:T(8,128)}, /*index=5*/f32[512,768]{1,0:T(8,128)}) custom-call(bf16[512,768]{1,0:T(8,128)(2,1)} %bitcast.18, bf16[512,768]{1,0:T(8,128)(2,1)} %bitcast.19, f32[2,24,3072]{2,1,0:T(8,128)} %attn_ref.1, ...), custom_call_target="tpu_custom_call" | custom-call | tf_op jit(solution)/shard_map/pallas_call | solution.py:1016
  166.8 0.7 copy.35
  167.5 0.0 copy-done.13
  167.5 0.0 copy-done.14
  167.5 0.0 copy-done.15
  167.5 0.7 multiply_subtract_fusion.3
  168.2 0.0 copy-done
  168.2 0.0 copy-done.5
  168.2 0.0 copy-done.6
  168.2 0.0 copy-start.1
  168.2 0.0 copy-start.7
  168.2 0.0 copy-start.8
  168.2 0.0 copy-start.12
  168.2 2.7 %multiply_subtract_fusion.2 = (f32[2,24,3072]{2,1,0:T(8,128)}, f32[2,24,3072]{2,1,0:T(8,128)}, f32[2,24,3072]{2,1,0:T(8,128)}) fusion(f32[2,24,3072]{2,1,0:T(8,128)S(1)} %copy-done, f32[2,24,3072]{2,1,0:T(8,128)} %get-tuple-element.20, f32[2,24,3072]{2,1,0:T(8,128)S(1)} %copy-done.5, f32[2,24,3072]{2,1,0:T(8,128)S(1)} %copy-done.6), kind=kLoop, calls=%fused_computation.10 | loop fusion | flops 2211840 | bytes 4128768 | tf_op jit(solution)/shard_map/sub | solution.py:239
  170.9 0.0 copy-done.1
  170.9 0.0 copy-done.7
  170.9 0.0 copy-done.8
  170.9 0.0 copy-done.12
  170.9 0.0 copy-start.2
  170.9 0.0 copy-start.9
  171.0 0.0 copy-start.10
  171.0 0.0 copy-start.11
  171.0 1.5 multiply_subtract_fusion.1
  172.5 0.0 copy-done.2
  172.5 0.0 copy-done.9
  172.5 0.5 copy-done.10
  173.0 0.2 copy-done.11
  173.2 0.0 copy-start.4
  173.2 1.5 multiply_subtract_fusion
  174.7 0.6 copy-done.4
  175.2 0.0 copy-start.3
  175.2 1.1 copy.40
  176.4 0.8 copy-done.3
  177.2 1.1 copy.41
  (5 shorter events, 0.0 us)
Async XLA Ops:
  5.2 162.2 %copy-start.13 = (f32[2,288]{1,0:T(2,128)S(1)}, f32[2,288]{1,0:T(2,128)}, u32[]{:S(2)}) copy-start(f32[2,288]{1,0:T(2,128)} %param.30) | copy-start | bytes 6916
  5.2 162.2 %copy-start.14 = (f32[2,288]{1,0:T(2,128)S(1)}, f32[2,288]{1,0:T(2,128)}, u32[]{:S(2)}) copy-start(f32[2,288]{1,0:T(2,128)} %param.32) | copy-start | bytes 6916
  5.2 162.2 %copy-start.15 = (f32[2,288]{1,0:T(2,128)S(1)}, f32[2,288]{1,0:T(2,128)}, u32[]{:S(2)}) copy-start(f32[2,288]{1,0:T(2,128)} %param.31) | copy-start | bytes 6916
  5.2 162.9 %copy-start = (f32[2,24,3072]{2,1,0:T(8,128)S(1)}, f32[2,24,3072]{2,1,0:T(8,128)}, u32[]{:S(2)}) copy-start(f32[2,24,3072]{2,1,0:T(8,128)} %attn_ref.1) | copy-start | bytes 1769476
  5.3 162.9 %copy-start.5 = (f32[2,24,3072]{2,1,0:T(8,128)S(1)}, f32[2,24,3072]{2,1,0:T(8,128)}, u32[]{:S(2)}) copy-start(f32[2,24,3072]{2,1,0:T(8,128)} %param.23) | copy-start | bytes 1769476
  5.3 162.9 %copy-start.6 = (f32[2,24,3072]{2,1,0:T(8,128)S(1)}, f32[2,24,3072]{2,1,0:T(8,128)}, u32[]{:S(2)}) copy-start(f32[2,24,3072]{2,1,0:T(8,128)} %param.22) | copy-start | bytes 1769476
  168.2 2.7 %copy-start.1 = (f32[2,24,3072]{2,1,0:T(8,128)S(1)}, f32[2,24,3072]{2,1,0:T(8,128)}, u32[]{:S(2)}) copy-start(f32[2,24,3072]{2,1,0:T(8,128)} %ffi_ref.1) | copy-start | bytes 1769476
  168.2 2.7 %copy-start.7 = (f32[2,24,3072]{2,1,0:T(8,128)S(1)}, f32[2,24,3072]{2,1,0:T(8,128)}, u32[]{:S(2)}) copy-start(f32[2,24,3072]{2,1,0:T(8,128)} %param.26) | copy-start | bytes 1769476
  168.2 2.7 %copy-start.8 = (f32[2,24,3072]{2,1,0:T(8,128)S(1)}, f32[2,24,3072]{2,1,0:T(8,128)}, u32[]{:S(2)}) copy-start(f32[2,24,3072]{2,1,0:T(8,128)} %param.25) | copy-start | bytes 1769476
  168.2 2.7 %copy-start.12 = (f32[2,24,3072]{2,1,0:T(8,128)S(1)}, f32[2,24,3072]{2,1,0:T(8,128)}, u32[]{:S(2)}) copy-start(f32[2,24,3072]{2,1,0:T(8,128)} %get-tuple-element.21) | copy-start | bytes 1769476
  170.9 1.5 copy-start.2
  170.9 1.5 copy-start.9
  171.0 2.0 %copy-start.10 = (f32[2,96,768]{2,1,0:T(8,128)S(1)}, f32[2,96,768]{2,1,0:T(8,128)}, u32[]{:S(2)}) copy-start(f32[2,96,768]{2,1,0:T(8,128)} %param.28) | copy-start | bytes 1769476
  171.0 2.2 %copy-start.11 = (f32[2,96,768]{2,1,0:T(8,128)S(1)}, f32[2,96,768]{2,1,0:T(8,128)}, u32[]{:S(2)}) copy-start(f32[2,96,768]{2,1,0:T(8,128)} %get-tuple-element.22) | copy-start | bytes 1769476
  173.2 2.0 %copy-start.4 = (f32[512,768]{1,0:T(8,128)S(1)}, f32[512,768]{1,0:T(8,128)}, u32[]{:S(2)}) copy-start(f32[512,768]{1,0:T(8,128)} %get-tuple-element.24) | copy-start | bytes 4718596
  175.2 2.0 %copy-start.3 = (f32[512,768]{1,0:T(8,128)S(1)}, f32[512,768]{1,0:T(8,128)}, u32[]{:S(2)}) copy-start(f32[512,768]{1,0:T(8,128)} %get-tuple-element.25) | copy-start | bytes 4718596

commit v2 on v1

--- a/solution.py
+++ b/solution.py
@@ -431,11 +431,11 @@
 
 
 def step_kernel(
-    qt_ref, pt_ref, attn_ref, ffi_ref, ffo_ref, small_ref, bnd_ref,
+    qt_ref, pt_ref, attn_ref, ffi_ref, ffo_ref, small_ref, len_ref, pos_ref,
     ga_ref, gi_ref, go_ref, gs_ref, dxq_ref, dxp_ref,
-    X, slabA, slabI, slabO, smb, bndb, R, WN, sn, sno, ST, Pf, Pb, DSb, Emat, b1p,
+    X, slabA, slabI, slabO, smw, sm2, smb, bndo, bndb, R, WN, sn, sno, ST, Pf, Pb, DSb, Emat, b1p,
     w1s_, w1r, W1, W2, Yb, P2s, P2r, XH, Dout, dZb, Gb, Act, P3s, P3r, Qb, dAb, dUb, dQb,
-    m1s, m1r, m2s, m2r, dws, dwr, sgs, sgr, GS, GSw, GA, GI, GO, DX, qsb, vtb, ybf,
+    m1s, m1r, m2s, m2r, dws, dwr, sgr, GS, GSw, GA, GI, GO, DX, qsb, vtb, ybf,
     loc, sib_s, sib_r, at_s, at_r, ag_s, ag_z, ag_p, aa_s, aa_r, out_l, out_s, out_r,
 ):
     dp, z = lax.axis_index("dp"), lax.axis_index("pair")
@@ -462,6 +462,9 @@
         pltpu.make_async_copy(ref, ref, sem).wait()
 
     barrier = pltpu.get_barrier_semaphore()
+    other = 1 - core
+    rows = pl.ds(pl.multiple_of(512 * core, 512), 512)
+    pltpu.make_async_copy(attn_ref.at[core], slabA.at[core], loc.at[0]).start()
 
     def greet(r, c):
         pl.semaphore_signal(
@@ -469,30 +472,58 @@
         )
         return c
 
+    pl.semaphore_signal(barrier, inc=1, device_id=sibling, device_id_type=MESH_ID)
     lax.fori_loop(1, 16, greet, 0)
-    pl.semaphore_signal(barrier, inc=1, device_id=sibling, device_id_type=MESH_ID)
-
-    rows = pl.ds(pl.multiple_of(512 * core, 512), 512)
-    pltpu.make_async_copy(attn_ref.at[core], slabA.at[core], loc.at[0]).start()
-    pltpu.make_async_copy(small_ref.at[core], smb.at[own, core], loc.at[1]).start()
-    pltpu.make_async_copy(bnd_ref.at[core], bndb.at[core], loc.at[2]).start()
 
     @pl.when(core == 0)
     def _():
-        pltpu.make_async_copy(qt_ref, X.at[rows], loc.at[3]).start()
+        pltpu.make_async_copy(qt_ref, X.at[rows], loc.at[1]).start()
 
     @pl.when(core == 1)
     def _():
-        pltpu.make_async_copy(pt_ref, X.at[rows], loc.at[3]).start()
-
-    pltpu.make_async_copy(ffi_ref.at[core], slabI.at[core], loc.at[4]).start()
-    pltpu.make_async_copy(ffo_ref.at[core], slabO.at[core], loc.at[5]).start()
+        pltpu.make_async_copy(pt_ref, X.at[rows], loc.at[1]).start()
+
+    pltpu.make_async_copy(ffi_ref.at[core], slabI.at[core], loc.at[2]).start()
+    pltpu.make_async_copy(ffo_ref.at[core], slabO.at[core], loc.at[3]).start()
+
+    narrow = small_ref[...].astype(LOW).astype(F32)
+    window = jnp.zeros((2, 384), F32)
+    for i in range(4):
+        gaps = [jnp.zeros((2, n), F32) for n in (32 * i, 96 - 32 * i) if n]
+        placed = jnp.concatenate(([gaps[0]] if i else []) + [narrow] + ([gaps[-1]] if i < 3 else []), axis=1)
+        window = jnp.where(z == i, placed, window)
+    for k in range(2):
+        smw[k] = jnp.concatenate(
+            [window[k : k + 1, 128 * i : 128 * i + 128] for i in range(3)]
+            + [jnp.zeros((5, 128), F32)], axis=0,
+        )
+    sm2[core] = smw[core]
+
+    lengths = len_ref[...].astype(F32)
+    spans = jnp.concatenate(
+        [jnp.broadcast_to(lengths[i : i + 1], (4, 4)) for i in range(2)], axis=0
+    )
+    at_row = lax.broadcasted_iota(jnp.int32, (8, 4), 0)
+    at_lane = lax.broadcasted_iota(jnp.int32, (8, 4), 1)
+    upto = at_lane <= lax.rem(at_row, 4)
+    here = at_lane == lax.rem(at_row, 4)
+    line_of = lax.broadcasted_iota(jnp.int32, (8, 1), 0)
+    base = jnp.where(line_of >= 4, 256.0, 0.0)
+    passage_end = jnp.sum(jnp.where(upto, spans, 0.0), axis=1, keepdims=True) + base
+    passage_start = passage_end - jnp.sum(jnp.where(here, spans, 0.0), axis=1, keepdims=True)
+    question_start = line_of.astype(F32) * 64.0
+    eye = lax.broadcasted_iota(jnp.int32, (8, 8), 0) == lax.broadcasted_iota(jnp.int32, (8, 8), 1)
+    goal = jnp.broadcast_to(pos_ref[...].astype(F32), (8, 8))
+    goal = jnp.sum(jnp.where(eye, goal, 0.0), axis=1, keepdims=True)
+    of_questions = jnp.concatenate([question_start, question_start + 64.0, goal], axis=0)
+    of_passages = jnp.concatenate([passage_start, passage_end, goal], axis=0)
+    bndb[core] = jnp.broadcast_to(jnp.where(core == 0, of_questions, of_passages), (24, 128))
+    bndo[...] = jnp.broadcast_to(jnp.where(core == 0, of_passages, of_questions), (24, 128))
     pl.semaphore_wait(barrier, 16)
 
-    other = 1 - core
+    remote(smw.at[other], sm2.at[core], sib_s.at[1], sib_r.at[1], sibling).start()
     remote(attn_ref.at[other], slabA.at[core], sib_s.at[0], sib_r.at[0], sibling).start()
-    remote(small_ref.at[other], smb.at[own, core], sib_s.at[1], sib_r.at[1], sibling).start()
-    remote(bnd_ref.at[other], bndb.at[core], sib_s.at[2], sib_r.at[2], sibling).start()
+    remote(bndo, bndb.at[core], sib_s.at[2], sib_r.at[2], sibling).start()
 
     @pl.when(core == 0)
     def _():
@@ -505,60 +536,134 @@
     remote(ffi_ref.at[other], slabI.at[core], sib_s.at[4], sib_r.at[4], sibling).start()
     remote(ffo_ref.at[other], slabO.at[core], sib_s.at[5], sib_r.at[5], sibling).start()
 
+    done(sm2.at[other], sib_r.at[1])
+    smb[own] = jnp.concatenate([sm2[0], sm2[1]], axis=0).astype(LOW)
+
+    exchanged = (smb, w1r, P2r, m1r, P3r, dwr, m2r)
+    gathered = (Yb, Qb, XH.at[core], dUb, dAb, dQb, sgr)
+    passed = ((slabA.at[0], slabA.at[0]), (sm2.at[0], sm2.at[0]), (bndb.at[0], bndb.at[0]),
+              (X.at[rows], X.at[rows]), (slabI.at[0], slabI.at[0]), (slabO.at[0], slabO.at[0]),
+              (sn, sno), (XH.at[0], XH.at[0]))
+    written = (GO.at[0], DX.at[rows], GI.at[0], GA.at[0], GSw.at[0])
+    state = {("pass", n): int(n < 2) for n in range(6)}
+
+    def direct(n, src_of):
+        def body(r, c):
+            target = lax.rem(own + r, 16)
+            remote(src_of(target), exchanged[n].at[own], aa_s.at[n], aa_r.at[n], dev(target, core)).start()
+            return c
+
+        lax.fori_loop(1, 16, body, 0)
+        state["direct", n] = 0
+
+    def direct_done(n):
+        done(exchanged[n].at[pl.ds(0, 15)], aa_r.at[n])
+        state["direct", n] = 1
+
+    def pass_done(n):
+        done(passed[n][1], sib_r.at[n])
+        state["pass", n] = 1
+
+    direct(0, lambda t: smb.at[own])
+
+    def push(slot, m, target):
+        remote(R.at[slot, m], R.at[slot, m], at_s.at[m], at_r.at[slot, m, 0], dev(target, core)).start()
+
+    def near(f, nearest=1):
+        for d in range(nearest, 4):
+            for dz in (d, -d) if d else (0,):
+                @pl.when(jnp.logical_and(z + dz >= 0, z + dz <= 3))
+                def _():
+                    f(dz)
+
+    def got(slot, m):
+        done(R.at[slot, m], at_r.at[slot, m, 0])
+
     done(slabA.at[core], loc.at[0])
     done(slabA.at[other], sib_r.at[0])
-    for m in range(4):
+    for m in (0, 3, 1, 2):
         cols = slice(768 * m, 768 * m + 768)
         R[own, m] = jnp.concatenate([slabA[0, :, cols], slabA[1, :, cols]], axis=0).astype(LOW)
-        for target in (slot_x, slot_y):
-            remote(R.at[own, m], R.at[own, m], at_s.at[m], at_r.at[own, m, 0], dev(target, core)).start()
-
-        def along_z(r, c):
-            target = line + lax.rem(z + r, 4)
-            remote(R.at[own, m], R.at[own, m], at_s.at[m], at_r.at[own, m, 0], dev(target, core)).start()
-            return c
-
-        lax.fori_loop(1, 4, along_z, 0)
-
-    done(smb.at[own, core], loc.at[1])
-    done(smb.at[own, other], sib_r.at[1])
-
-    def direct(src_of, dst, ssem, rsem):
-        def body(r, c):
-            target = lax.rem(own + r, 16)
-            remote(src_of(target), dst.at[own], ssem, rsem, dev(target, core)).start()
-            return c
-
-        lax.fori_loop(1, 16, body, 0)
-
-    def direct_done(dst, rsem):
-        done(dst.at[pl.ds(0, 15)], rsem)
-
-    direct(lambda t: smb.at[own], smb, aa_s.at[0], aa_r.at[0])
+        for target in (slot_x, slot_y) if m < 3 else (slot_x, slot_y, slot_d):
+            push(own, m, target)
+        if m < 3:
+            near(lambda dz: push(own, m, own + dz))
+
+    def hop(d):
+        for i in range(4):
+            slot = 4 * i + z
+            if d == 0:
+                @pl.when(4 * i != line)
+                def _():
+                    got(slot, 3)
+
+                @pl.when(z < 3)
+                def _():
+                    push(slot, 3, own + 1)
+
+                @pl.when(z > 0)
+                def _():
+                    push(slot, 3, own - 1)
+            else:
+                @pl.when(z - d >= 0)
+                def _():
+                    got(slot - d, 3)
+
+                    @pl.when(z < 3)
+                    def _():
+                        push(slot - d, 3, own + 1)
+
+                @pl.when(z + d <= 3)
+                def _():
+                    got(slot + d, 3)
+
+                    @pl.when(z > 0)
+                    def _():
+                        push(slot + d, 3, own - 1)
+
+    def finish():
+        for kind, n in list(state):
+            if kind == "gather" and state[kind, n] == 0:
+                gather_forward(n)
+            if kind == "gather" and state[kind, n] == 1:
+                gather_done(n)
+            if kind == "direct" and state[kind, n] == 0:
+                direct_done(n)
+            if kind == "pass" and state[kind, n] == 0:
+                pass_done(n)
+            if kind == "gather":
+                done(gathered[n].at[pl.ds(0, 15)], ag_s.at[n])
+            if kind == "direct":
+                done(exchanged[n].at[pl.ds(0, 15)], aa_s.at[n])
+            if kind == "pass":
+                done(passed[n][0], sib_s.at[n])
+            if kind == "out":
+                done(written[n], out_l.at[n])
+                done(written[n], out_s.at[n])
+                done(written[n], out_r.at[n])
+        for m in range(3):
+            done(R.at[pl.ds(0, 15), m], at_s.at[m])
+        done(R.at[pl.ds(0, 7), 3], at_s.at[3])
+
+        @pl.when(jnp.logical_and(z > 0, z < 3))
+        def _():
+            done(R.at[pl.ds(0, 16), 3], at_s.at[3])
 
     def relay(m):
-        def from_z(r, c):
-            slot = line + lax.rem(z + r, 4)
-            done(R.at[slot, m], at_r.at[slot, m, 0])
+        def from_z(dz):
+            got(own + dz, m)
             for target in (slot_x, slot_y):
-                remote(R.at[slot, m], R.at[slot, m], at_s.at[m], at_r.at[slot, m, 0], dev(target, core)).start()
-            return c
-
-        lax.fori_loop(1, 4, from_z, 0)
-
-        def from_plane(r, c):
-            zz = lax.rem(z + r, 4)
-            for base, target, half in (
-                (y * 8 + (1 - x) * 4, slot_y, 0),
-                ((1 - y) * 8 + x * 4, slot_x, 1),
-            ):
-                slot = base + zz
-                done(R.at[slot, m], at_r.at[slot, m, 0])
+                push(own + dz, m, target)
+
+        near(from_z)
+
+        def from_plane(dz):
+            for slot, target, half in ((slot_x + dz, slot_y, 0), (slot_y + dz, slot_x, 1)):
+                got(slot, m)
                 part = R.at[slot, m, :, pl.ds(384 * half, 384)]
                 remote(part, part, at_s.at[m], at_r.at[slot, m, half], dev(target, core)).start()
-            return c
-
-        lax.fori_loop(0, 4, from_plane, 0)
+
+        near(from_plane, 0)
 
     def from_slots(read, write):
         def body(g, c):
@@ -588,36 +693,47 @@
                 done(R.at[slot, m, :, pl.ds(384 * half, 384)], at_r.at[slot, m, half])
             return c
 
-        lax.fori_loop(0, 4, body, 0)
+        if m < 3:
+            lax.fori_loop(0, 4, body, 0)
 
         def write(where, v):
             WN[m, where, :] = v
 
         from_slots(lambda s: R[s, m], write)
 
-    def gather_start(buf, n):
-        def body(r, c):
-            target = line + lax.rem(z + r, 4)
-            remote(buf.at[own], buf.at[own], ag_s.at[n], ag_z.at[n], dev(target, core)).start()
-            return c
-
-        lax.fori_loop(1, 4, body, 0)
-
-    def gather_forward(buf, n):
-        done(buf.at[pl.ds(0, 3)], ag_z.at[n])
-        block = buf.at[pl.ds(line, 4)]
+    def gather_start(n):
+        buf = gathered[n]
+        state["gather", n] = 0
+
+        def give(dz):
+            remote(buf.at[own], buf.at[own], ag_s.at[n], ag_z.at[n, z], dev(own + dz, core)).start()
+
+        near(give)
         for target in (slot_x, slot_y, slot_d):
-            remote(block, block, ag_s.at[n], ag_p.at[n], dev(target, core)).start()
-
-    def gather_done(buf, n):
-        done(buf.at[pl.ds(0, 12)], ag_p.at[n])
+            remote(buf.at[own], buf.at[own], ag_s.at[n], ag_p.at[n], dev(target, core)).start()
+
+    def gather_forward(n):
+        buf = gathered[n]
+        state["gather", n] = 1
+
+        def pass_on(dz):
+            block = buf.at[own + dz]
+            done(block, ag_z.at[n, z + dz])
+            for target in (slot_x, slot_y, slot_d):
+                remote(block, block, ag_s.at[n], ag_p.at[n], dev(target, core)).start()
+
+        near(pass_on)
+
+    def gather_done(n):
+        state["gather", n] = 2
+        done(gathered[n].at[pl.ds(0, 12)], ag_p.at[n])
 
     def prepare_ffn():
         row = lax.broadcasted_iota(jnp.int32, (384, 512), 0)
         col = lax.broadcasted_iota(jnp.int32, (384, 512), 1)
         Emat[...] = jnp.where(col == 128 * (row // 96) + lax.rem(row, 96), 1.0, 0.0).astype(LOW)
-        done(slabI.at[core], loc.at[4])
-        done(slabI.at[other], sib_r.at[4])
+        done(slabI.at[core], loc.at[2])
+        pass_done(4)
         for g in range(8):
             cols = slice(384 * g, 384 * g + 384)
             part = jnp.concatenate([slabI[0, :, cols], slabI[1, :, cols]], axis=0).astype(LOW)
@@ -626,45 +742,52 @@
                 w1s_[4 * (g // 2) + i, :, 128 * (g % 2) : 128 * (g % 2) + 128] = wide[
                     :, 128 * i : 128 * i + 128
                 ]
-        direct(lambda t: w1s_.at[t], w1r, aa_s.at[1], aa_r.at[1])
         w1r[own] = w1s_[own]
-        done(slabO.at[core], loc.at[5])
-        done(slabO.at[other], sib_r.at[5])
+        done(slabO.at[core], loc.at[3])
+        pass_done(5)
         gap = jnp.zeros((32, 768), F32)
         W2[...] = jnp.concatenate([slabO[0], gap, slabO[1], gap], axis=0).astype(LOW)
 
     def natural_small():
-        direct_done(smb, aa_r.at[0])
+        direct_done(0)
         for g in range(8):
-            parts = [smb[4 * (g // 2) + i, g % 2] for i in range(4)]
+            parts = [
+                smb[4 * (g // 2) + i].astype(F32)[8 * (g % 2) : 8 * (g % 2) + 8] for i in range(4)
+            ]
             lines = [parts[0][0:1], parts[0][1:2]]
             for i in range(1, 4):
                 lines += [parts[i - 1][2:3] + parts[i][0:1], parts[i][1:2]]
             lines += [parts[3][2:3]]
             sn[9 * g : 9 * g + 9, :] = jnp.concatenate(lines, axis=0)
         remote(sn, sno, sib_s.at[6], sib_r.at[6], sibling).start()
+        state["pass", 6] = 0
 
     def vec(row, count=6, ref=sn):
         return jnp.concatenate([ref[row + i : row + i + 1, :] for i in range(count)], axis=1)
 
     relay(0)
-    done(bndb.at[core], loc.at[2])
-    done(bndb.at[other], sib_r.at[2])
-    done(X.at[pl.ds(0, 512)], loc.at[3])
-    done(X.at[pl.ds(0, 512)], sib_r.at[3])
-    starts = jnp.concatenate([bndb[0, 0:8], bndb[1, 0:8] + 512], axis=0)[:, 0:1]
-    ends = jnp.concatenate([bndb[0, 8:16], bndb[1, 8:16] + 512], axis=0)[:, 0:1]
-    token = lax.broadcasted_iota(jnp.int32, (16, 1024), 1)
+    hop(0)
+    pass_done(2)
+    done(X.at[pl.ds(0, 512)], loc.at[1])
+    pass_done(3)
+    starts = jnp.concatenate([bndb[0, 0:8], bndb[1, 0:8] + 512.0], axis=0)[:, 0:1]
+    ends = jnp.concatenate([bndb[0, 8:16], bndb[1, 8:16] + 512.0], axis=0)[:, 0:1]
+    token = lax.broadcasted_iota(jnp.int32, (16, 1024), 1).astype(F32)
     inside = jnp.logical_and(token >= starts, token < ends)
     first = jnp.where(token == starts, 1.0, 0.0).astype(LOW)
     cls_in = dot_nn(first, X[...])
     cls_low = cls_in.astype(LOW)
     natural_small()
+    prepare_ffn()
     relay(1)
+    hop(1)
     arrive(0)
     queries = (dot_nn(cls_low, WN[0]) + vec(0)).astype(LOW)
     Qb[own] = queries
     relay(2)
+    hop(2)
+    direct(1, lambda t: w1s_.at[t])
+    gather_start(1)
     arrive(1)
     qsb[...] = (dot_nt(expand_heads(queries), WN[1]) * (HD**-0.5)).astype(LOW)
     ST[...] = dot_nt(qsb[...], X[...])
@@ -679,11 +802,10 @@
         return c
 
     lax.fori_loop(0, 12, soften, 0)
-    relay(3)
     ybf[...] = dot_nn(Pb[...], X[...]).astype(LOW)
-    prepare_ffn()
     arrive(2)
     mixed = (pick_heads(dot_nn(ybf[...], WN[2])) + vec(6)).astype(LOW)
+    hop(3)
     arrive(3)
     lifted = cls_in + dot_nn(mixed, WN[3]) + vec(12)
     centred = lifted - jnp.mean(lifted, axis=1, keepdims=True)
@@ -691,8 +813,7 @@
     hat_one = centred * rstd_one
     normed = hat_one * vec(18) + vec(24)
     Yb[own] = normed.astype(LOW)
-    gather_start(Yb, 0)
-    gather_start(Qb, 1)
+    gather_start(0)
 
     early = jnp.concatenate(
         [ybf[...].astype(F32), cls_in, mixed.astype(F32), jnp.zeros((32, 768), F32)], axis=0
@@ -704,7 +825,7 @@
 
     to_slots(lambda w: DX[w, 0:256], write_m1)
     m1r[own] = m1s[own]
-    gather_forward(Yb, 0)
+    gather_forward(0)
 
     b1 = jnp.concatenate([vec(30 + 3 * g, 3) for g in range(8)], axis=0).astype(LOW)
     b1_wide = dot_nn(b1, Emat[...])
@@ -715,43 +836,43 @@
     b1_row = jnp.concatenate(
         [b1p[gy, 0:1, pl.ds(group, 128)], b1p[gy + 1, 0:1, pl.ds(group, 128)]], axis=1
     )
-    direct_done(w1r, aa_r.at[1])
+    direct_done(1)
 
     def write_w1(where, v):
         W1[where, :] = v
 
     from_slots(lambda s: w1r[s], write_w1)
-    gather_done(Yb, 0)
+    gather_done(0)
     all_y = Yb[...].reshape(256, 768)
     act = dot_nn(all_y, W1[...]) + b1_row
     Act[...] = act
     hidden, unused = gelu_parts(act)
     Gb[...] = hidden.astype(LOW)
     P2s[...] = dot_nn(Gb[...], W2[...]).astype(LOW).reshape(16, 16, 768)
-    direct(lambda t: P2s.at[t], P2r, aa_s.at[2], aa_r.at[2])
+    direct(2, lambda t: P2s.at[t])
     P2r[own] = P2s[own]
-    gather_forward(Qb, 1)
-    direct_done(P2r, aa_r.at[2])
-    direct(lambda t: m1s.at[t], m1r, aa_s.at[3], aa_r.at[3])
+    gather_forward(1)
+    direct_done(2)
     second = normed + jnp.sum(P2r[...].astype(F32), axis=0) + vec(54)
     centred = second - jnp.mean(second, axis=1, keepdims=True)
     rstd_two = lax.rsqrt(jnp.mean(centred * centred, axis=1, keepdims=True) + NORM_EPS)
     hat_two = centred * rstd_two
     rstd_high, rstd_low = split_low(rstd_two)
     lane = lax.broadcasted_iota(jnp.int32, (16, 128), 1)
-    positive = jnp.concatenate([bndb[0, 16:24], bndb[1, 16:24]], axis=0).astype(F32)
+    positive = jnp.concatenate([bndb[0, 16:24], bndb[1, 16:24]], axis=0)
     extra = jnp.where(
         lane == 0, rstd_high.astype(F32),
         jnp.where(lane == 1, rstd_low.astype(F32), jnp.where(lane == 2, positive, 0.0)),
     )
     XH[core, own] = jnp.concatenate([hat_two, extra], axis=1).astype(LOW)
-    mine = XH.at[core]
-    gather_start(mine, 2)
-    gather_forward(mine, 2)
-    gather_done(mine, 2)
+    gather_start(2)
+    gather_forward(2)
+    direct(3, lambda t: m1s.at[t])
+    gather_done(2)
     remote(XH.at[core], XH.at[core], sib_s.at[7], sib_r.at[7], sibling).start()
-    done(sno, sib_r.at[6])
-    done(XH.at[other], sib_r.at[7])
+    state["pass", 7] = 0
+    pass_done(6)
+    pass_done(7)
 
     def vec_of(encoder, row):
         return jnp.where(core == encoder, vec(row), vec(row, 6, sno))
@@ -799,23 +920,25 @@
     unused, slope = gelu_parts(Act[...])
     da = (dot_nt(dZb[...], W2[...]) * slope).astype(LOW)
     P3s[...] = dot_nt(da, W1[...]).astype(LOW).reshape(16, 16, 768)
-    direct(lambda t: P3s.at[t], P3r, aa_s.at[4], aa_r.at[4])
+    direct(4, lambda t: P3s.at[t])
     P3r[own] = P3s[own]
+    DX[0:768, 0:256] = dot_tn(all_y, da)
+
+    def write_dw(slot, v):
+        dws[slot] = v
+
+    to_slots(lambda w: DX[w, 0:256], write_dw)
+    direct(5, lambda t: dws.at[t])
+    dwr[own] = dws[own]
     db1 = jnp.sum(da.astype(F32), axis=0, keepdims=True)
     dw2 = dot_tn(Gb[...], dZb[...])
     GO[0] = dw2[0:96]
     GO[1] = dw2[128:224]
     pltpu.make_async_copy(GO.at[core], go_ref.at[core], out_l.at[0]).start()
     remote(GO.at[other], go_ref.at[core], out_s.at[0], out_r.at[0], sibling).start()
-    DX[0:768, 0:256] = dot_tn(all_y, da)
-
-    def write_dw(slot, v):
-        dws[slot] = v
-
-    to_slots(lambda w: DX[w, 0:256], write_dw)
-    dwr[own] = dws[own]
+    state["out", 0] = 0
     own_rows = pl.ds(pl.multiple_of(16 * own, 16), 16)
-    direct_done(P3r, aa_r.at[4])
+    direct_done(4)
 
     grad_normed = Dout[own_rows, :] + jnp.sum(P3r[...].astype(F32), axis=0)
     inner = grad_normed * vec(18)
@@ -827,22 +950,23 @@
     grad_mixed = dot_nt(grad_lift, WN[3]).astype(LOW)
     dUb[own] = grad_lift
     dAb[own] = grad_mixed
-    gather_start(dUb, 3)
-    gather_start(dAb, 4)
-    direct(lambda t: dws.at[t], dwr, aa_s.at[5], aa_r.at[5])
+    gather_start(3)
+    gather_start(4)
     dg1 = jnp.sum(grad_normed * hat_one, axis=0, keepdims=True)
     ds1 = jnp.sum(grad_normed, axis=0, keepdims=True)
-    sgs[...] = jnp.concatenate(
+    sgr[own] = jnp.concatenate(
         [dg1[:, 128 * i : 128 * i + 128] for i in range(6)]
         + [ds1[:, 128 * i : 128 * i + 128] for i in range(6)]
         + [db1[:, 0:128], db1[:, 128:256], jnp.zeros((2, 128), F32)], axis=0,
     )
-    direct(lambda t: sgs, sgr, aa_s.at[6], aa_r.at[6])
-    sgr[own] = sgs[...]
+    gather_start(6)
     spread = expand_heads(grad_mixed)
     vtb[...] = dot_nt(spread, WN[2]).astype(LOW)
     constant = jnp.sum(spread.astype(F32) * vec(6), axis=1, keepdims=True)
     ST[...] = dot_nt(vtb[...], X[...]) + constant
+    gather_forward(3)
+    gather_forward(4)
+    gather_forward(6)
 
     def harden(h, c):
         at = pl.ds(pl.multiple_of(16 * h, 16), 16)
@@ -861,14 +985,11 @@
         m2s[slot] = v
 
     to_slots(lambda w: DX[w, 0:256], write_m2)
-    direct(lambda t: m2s.at[t], m2r, aa_s.at[7], aa_r.at[7])
+    direct(6, lambda t: m2s.at[t])
     m2r[own] = m2s[own]
     grad_query = pick_heads(dot_nn(late, WN[1])).astype(LOW)
     dQb[own] = grad_query
-    gather_start(dQb, 5)
-    gather_forward(dUb, 3)
-    gather_forward(dAb, 4)
-    gather_forward(dQb, 5)
+    gather_start(5)
 
     grad_cls = grad_one + dot_nt(grad_query, WN[0])
     cls_high, cls_rest = split_low(grad_cls)
@@ -877,6 +998,7 @@
         part = slice(512 * k, 512 * k + 512)
         left = jnp.concatenate([DSb[:, part], Pb[:, part], first[:, part], first[:, part]], axis=0)
         DX[part, :] = dot_tn(left, right)
+    gather_forward(5)
     other_rows = pl.ds(pl.multiple_of(512 * other, 512), 512)
 
     @pl.when(core == 0)
@@ -889,7 +1011,9 @@
         pltpu.make_async_copy(DX.at[rows], dxp_ref, out_l.at[1]).start()
         remote(DX.at[other_rows], dxp_ref, out_s.at[1], out_r.at[1], sibling).start()
 
-    direct_done(dwr, aa_r.at[5])
+    state["out", 1] = 0
+
+    direct_done(5)
     for g in range(8):
         wide = jnp.concatenate(
             [dwr[4 * (g // 2) + i, :, 128 * (g % 2) : 128 * (g % 2) + 128] for i in range(4)], axis=1
@@ -899,6 +1023,7 @@
         GI[1, :, 384 * g : 384 * g + 384] = narrow[24:48]
     pltpu.make_async_copy(GI.at[core], gi_ref.at[core], out_l.at[2]).start()
     remote(GI.at[other], gi_ref.at[core], out_s.at[2], out_r.at[2], sibling).start()
+    state["out", 2] = 0
 
     def put(m, v):
         GA[0, :, 768 * m : 768 * m + 768] = v[0:24]
@@ -913,11 +1038,11 @@
 
         return lax.fori_loop(0, 16, body, jnp.zeros((48, 768), F32))
 
-    gather_done(Qb, 1)
-    gather_done(dAb, 4)
-    direct_done(m1r, aa_r.at[3])
+    gather_done(1)
+    gather_done(4)
+    direct_done(3)
     put(2, factor_sum(m1r, dAb))
-    gather_done(dUb, 3)
+    gather_done(3)
 
     def columns_of(at):
         return jnp.concatenate(
@@ -926,15 +1051,16 @@
 
     all_du = dUb[...].reshape(256, 768)
     put(3, dot_nn(columns_of(208), all_du))
-    direct_done(m2r, aa_r.at[7])
+    direct_done(6)
     put(1, factor_sum(m2r, Qb))
-    gather_done(dQb, 5)
+    gather_done(5)
     all_dq = dQb[...].reshape(256, 768)
     put(0, dot_nn(columns_of(192), all_dq))
     pltpu.make_async_copy(GA.at[core], ga_ref.at[core], out_l.at[3]).start()
     remote(GA.at[other], ga_ref.at[core], out_s.at[3], out_r.at[3], sibling).start()
-
-    direct_done(sgr, aa_r.at[6])
+    state["out", 3] = 0
+
+    gather_done(6)
     sums = jnp.sum(sgr[...], axis=0)
     hidden_rows = []
     for g in range(8):
@@ -966,34 +1092,20 @@
         GSw[k] = GS[gy + k, z]
     pltpu.make_async_copy(GSw.at[core], gs_ref.at[core], out_l.at[4]).start()
     remote(GSw.at[other], gs_ref.at[core], out_s.at[4], out_r.at[4], sibling).start()
-
-    for n, (mine_ref, theirs) in enumerate(
-        ((GO.at[0], GO.at[0]), (DX.at[rows], DX.at[rows]), (GI.at[0], GI.at[0]),
-         (GA.at[0], GA.at[0]), (GSw.at[0], GSw.at[0]))
-    ):
-        done(mine_ref, out_l.at[n])
-        done(theirs, out_s.at[n])
-        done(theirs, out_r.at[n])
-    for n, ref in enumerate(
-        (slabA.at[0], smb.at[0, 0], bndb.at[0], X.at[rows], slabI.at[0], slabO.at[0], sn, XH.at[0])
-    ):
-        done(ref, sib_s.at[n])
-    for m in range(4):
-        done(R.at[pl.ds(0, 15), m], at_s.at[m])
-    for n, ref in enumerate((Yb, Qb, XH.at[0], dUb, dAb, dQb)):
-        done(ref.at[pl.ds(0, 15)], ag_s.at[n])
-    for n, ref in enumerate((smb, w1r, P2r, m1r, P3r, dwr, sgr, m2r)):
-        done(ref.at[pl.ds(0, 15)], aa_s.at[n])
-
-
-def kernel_call(qt, pt, attn, ffi, ffo, small, bnd):
+    state["out", 4] = 0
+
+    finish()
+
+
+def kernel_call(qt, pt, attn, ffi, ffo, small, lengths, positives):
     any_space = pl.BlockSpec(memory_space=pl.ANY)
     vmem = pl.BlockSpec(memory_space=pltpu.VMEM)
     V = pltpu.VMEM
     dma = pltpu.SemaphoreType.DMA
     scratch = [
         V((1024, 768), LOW), V((2, 24, 3072), F32), V((2, 24, 3072), F32), V((2, 96, 768), F32),
-        V((16, 2, 8, 128), F32), V((2, 24, 128), jnp.int32), V((16, 4, 48, 768), LOW),
+        V((2, 8, 128), F32), V((2, 8, 128), F32), V((16, 16, 128), LOW),
+        V((24, 128), F32), V((2, 24, 128), F32), V((16, 4, 48, 768), LOW),
         V((4, 768, 768), LOW), V((72, 128), F32), V((72, 128), F32), V((192, 1024), F32),
         V((192, 1024), F32), V((192, 1024), LOW), V((192, 1024), LOW), V((384, 512), LOW),
         V((8, 8, 512), F32),
@@ -1003,12 +1115,12 @@
         V((256, 256), F32), V((16, 16, 768), LOW), V((16, 16, 768), LOW), V((16, 16, 768), LOW),
         V((16, 16, 768), LOW), V((16, 16, 768), LOW), V((16, 16, 768), LOW),
         V((16, 48, 256), LOW), V((16, 48, 256), LOW), V((16, 48, 256), LOW), V((16, 48, 256), LOW),
-        V((16, 48, 256), LOW), V((16, 48, 256), LOW), V((16, 128), F32), V((16, 16, 128), F32),
+        V((16, 48, 256), LOW), V((16, 48, 256), LOW), V((16, 16, 128), F32),
         V((8, 4, 8, 128), F32), V((2, 8, 128), F32), V((2, 24, 3072), F32), V((2, 24, 3072), F32),
         V((2, 96, 768), F32), V((1024, 768), F32), V((192, 768), LOW), V((192, 768), LOW),
         V((192, 768), LOW),
-        dma((6,)), dma((8,)), dma((8,)), dma((4,)), dma((16, 4, 2)), dma((6,)), dma((6,)),
-        dma((6,)), dma((8,)), dma((8,)), dma((5,)), dma((5,)), dma((5,)),
+        dma((4,)), dma((8,)), dma((8,)), dma((4,)), dma((16, 4, 2)), dma((7,)), dma((7, 4)),
+        dma((7,)), dma((7,)), dma((7,)), dma((5,)), dma((5,)), dma((5,)),
     ]
     shapes = (
         (2, 24, 3072), (2, 24, 3072), (2, 96, 768), (2, 8, 128), (512, 768), (512, 768)
@@ -1016,13 +1128,61 @@
     return pl.pallas_call(
         step_kernel,
         out_shape=[jax.ShapeDtypeStruct(s, F32) for s in shapes],
-        in_specs=[any_space] * 5 + [vmem] * 2,
+        in_specs=[any_space] * 5 + [vmem] * 3,
         out_specs=[any_space] * 6,
         scratch_shapes=scratch,
         compiler_params=pltpu.CompilerParams(
             collective_id=0, has_side_effects=True, vmem_limit_bytes=56 << 20
         ),
-    )(qt, pt, attn, ffi, ffo, small, bnd)
+    )(qt, pt, attn, ffi, ffo, small, lengths, positives)
+
+
+def update_kernel(*refs):
+    ins, outs = refs[:18], refs[18:]
+    for n in range(3):
+        weight, first, second, grad = (r[...] for r in ins[4 * n : 4 * n + 4])
+        new = adam_update(weight, first, second, grad, RATE_MATRIX, DECAY_MATRIX)
+        for ref, value in zip(outs[3 * n : 3 * n + 3], new):
+            ref[...] = value
+
+    @pl.when(pl.program_id(0) == 0)
+    def _():
+        z = lax.axis_index("pair")
+        weight, first, second, window = ins[12:16]
+        lines = []
+        for e in range(2):
+            row = jnp.concatenate([window[e, i : i + 1, :] for i in range(3)], axis=1)
+            picked = row[:, 0:288]
+            for i in range(1, 4):
+                picked = jnp.where(z == i, row[:, 32 * i : 32 * i + 288], picked)
+            lines.append(picked)
+        grad = jnp.concatenate(lines, axis=0)
+        new = adam_update(weight[...], first[...], second[...], grad, RATE_SMALL, 0.0)
+        for ref, value in zip(outs[9:12], new):
+            ref[...] = value
+
+    outs[12][...] = ins[16][...]
+    outs[13][...] = ins[17][...]
+
+
+def update_call(attn, inner, outer, small, grad_question, grad_passage):
+    wide = pl.BlockSpec((1, 24, 768), lambda i: (i // 4, 0, i % 4))
+    tall = pl.BlockSpec((1, 24, 768), lambda i: (i // 4, i % 4, 0))
+    vector = pl.BlockSpec((2, 288), lambda i: (0, 0))
+    window = pl.BlockSpec((2, 8, 128), lambda i: (0, 0, 0))
+    token = pl.BlockSpec((64, 768), lambda i: (i, 0))
+
+    def like(a):
+        return jax.ShapeDtypeStruct(a.shape, F32)
+
+    return pl.pallas_call(
+        update_kernel,
+        grid=(8,),
+        out_shape=[like(g[0]) for g in (attn, inner, outer, small) for _ in range(3)]
+        + [like(grad_question), like(grad_passage)],
+        in_specs=[wide] * 8 + [tall] * 4 + [vector] * 3 + [window, token, token],
+        out_specs=[wide] * 6 + [tall] * 3 + [vector] * 3 + [token, token],
+    )(*attn, *inner, *outer, *small, grad_question, grad_passage)
 
 
 def local_kernel(
@@ -1030,35 +1190,23 @@
     attn_weight, attn_first, attn_second, ffn_in_weight, ffn_in_first, ffn_in_second,
     ffn_out_weight, ffn_out_first, ffn_out_second, small_params, small_first, small_second,
 ):
-    pair = lax.axis_index("pair")
-    zero = jnp.zeros((), jnp.int32)
-    low_small = small_params.astype(LOW).astype(F32)
-    window = lax.dynamic_update_slice(jnp.zeros((2, 1024), F32), low_small, (zero, 32 * pair))
-    ends = jnp.cumsum(passage_lengths, axis=1)
-    base = jnp.array([[0], [256]], jnp.int32)
-    passage_ends = (ends + base).reshape(8)
-    passage_starts = (ends - passage_lengths + base).reshape(8)
-    question_starts = jnp.arange(8, dtype=jnp.int32) * 64
-    marks = jnp.stack(
-        [
-            jnp.concatenate([question_starts, question_starts + 64, positives]),
-            jnp.concatenate([passage_starts, passage_ends, positives]),
-        ]
-    )
-    bounds = jnp.broadcast_to(marks[:, :, None], (2, 24, 128))
     grads = kernel_call(
         question_tokens.reshape(512, 768), passage_tokens.reshape(512, 768),
-        attn_weight, ffn_in_weight, ffn_out_weight, window.reshape(2, 8, 128), bounds,
+        attn_weight, ffn_in_weight, ffn_out_weight, small_params,
+        passage_lengths, positives.reshape(1, 8),
     )
     attn_sum, inner_sum, outer_sum, small_window, grad_question, grad_passage = grads
-    small_sum = lax.dynamic_slice(small_window.reshape(2, 1024), (zero, 32 * pair), (2, 288))
+    results = update_call(
+        (attn_weight, attn_first, attn_second, attn_sum),
+        (ffn_in_weight, ffn_in_first, ffn_in_second, inner_sum),
+        (ffn_out_weight, ffn_out_first, ffn_out_second, outer_sum),
+        (small_params, small_first, small_second, small_window),
+        grad_question, grad_passage,
+    )
     return (
-        *adam_update(attn_weight, attn_first, attn_second, attn_sum, RATE_MATRIX, DECAY_MATRIX),
-        *adam_update(ffn_in_weight, ffn_in_first, ffn_in_second, inner_sum, RATE_MATRIX, DECAY_MATRIX),
-        *adam_update(ffn_out_weight, ffn_out_first, ffn_out_second, outer_sum, RATE_MATRIX, DECAY_MATRIX),
-        *adam_update(small_params, small_first, small_second, small_sum, RATE_SMALL, 0.0),
-        grad_question.reshape(question_tokens.shape),
-        grad_passage.reshape(passage_tokens.shape),
+        *results[:12],
+        results[12].reshape(question_tokens.shape),
+        results[13].reshape(passage_tokens.shape),
     )
 
 

time: 179 us -> 148 us (0.83)
  Pallas kernels: 161 us -> 147 us
  other arithmetic: 9.41 us -> 0 us
  local copies, waits for them, and re-layouts: 6.67 us -> 0 us
    pallas_call x1, Pallas kernels: 161 us -> 136 us  [kernel_call(): pl.pallas_call(step_kernel, out_shape=[jax.ShapeDtypeStruct(s, F32) for s...]
    pallas_call x0 -> x1, Pallas kernels: none -> 10.5 us  [update_call(): pl.pallas_call(update_kernel, grid=(8,), out_shape=[like(g[0]) for g in (...]
    sub x4 -> x0, other arithmetic: 6.37 us -> none  [adam_update(): weight - step_rate * (update + decay_rate * weight)]
    unnamed x36 -> x0, local copies, waits for them, and re-layouts: 5.74 us -> none
where the time goes in v2:
time: 148 us
  Pallas kernels  147 us (99%)
    pallas_call x1, Pallas kernels, kernel_call(): pl.pallas_call(step_kernel, out_shape=[jax.ShapeDtypeStruct(s, F32) for s...  136 us
    pallas_call x1, Pallas kernels, update_call(): pl.pallas_call(update_kernel, grid=(8,), out_shape=[like(g[0]) for g in (...  10.5 us

profile of v2, /device:TPU:0, one launch (start us, length us, event | category | flops | bytes accessed | tf_op | source)
XLA Modules:
  0.0 147.6 jit_solution(3754119992024824216)
XLA Ops:
  0.6 136.3 %shard_map.263 = (f32[2,24,3072]{2,1,0:T(8,128)}, f32[2,24,3072]{2,1,0:T(8,128)}, f32[2,96,768]{2,1,0:T(8,128)}, f32[2,8,128]{2,1,0:T(8,128)}, f32[512,768]{1,0:T(8,128)}, /*index=5*/f32[512,768]{1,0:T(8,128)}) custom-call(bf16[512,768]{1,0:T(8,128)(2,1)} %bitcast.5, bf16[512,768]{1,0:T(8,128)(2,1)} %bitcast.6, f32[2,24,3072]{2,1,0:T(8,128)} %refs_0_.1, ...), custom_call_target="tpu_custom_call" | custom-call | tf_op jit(solution)/shard_map/pallas_call | solution.py:1128
  136.9 10.5 %shard_map.264 = (f32[2,24,3072]{2,1,0:T(8,128)}, f32[2,24,3072]{2,1,0:T(8,128)}, f32[2,24,3072]{2,1,0:T(8,128)}, f32[2,24,3072]{2,1,0:T(8,128)}, f32[2,24,3072]...) custom-call(f32[2,24,3072]{2,1,0:T(8,128)} %refs_0_.1, ...), custom_call_target="tpu_custom_call" | custom-call | tf_op jit(solution)/shard_map/pallas_call | solution.py:1178

commit v3 on v2

--- a/solution.py
+++ b/solution.py
@@ -434,9 +434,9 @@
     qt_ref, pt_ref, attn_ref, ffi_ref, ffo_ref, small_ref, len_ref, pos_ref,
     ga_ref, gi_ref, go_ref, gs_ref, dxq_ref, dxp_ref,
     X, slabA, slabI, slabO, smw, sm2, smb, bndo, bndb, R, WN, sn, sno, ST, Pf, Pb, DSb, Emat, b1p,
-    w1s_, w1r, W1, W2, Yb, P2s, P2r, XH, Dout, dZb, Gb, Act, P3s, P3r, Qb, dAb, dUb, dQb,
-    m1s, m1r, m2s, m2r, dws, dwr, sgr, GS, GSw, GA, GI, GO, DX, qsb, vtb, ybf,
-    loc, sib_s, sib_r, at_s, at_r, ag_s, ag_z, ag_p, aa_s, aa_r, out_l, out_s, out_r,
+    w1s_, w1r, W1, W2, Yb, P2s, P2a, P2b, P2c, XH, Dout, dZb, Gb, Act, P3s, P3a, P3b, P3c, Qb, dAb, dUb, dQb,
+    m1s, m1r, m2s, m2r, dws, dwr, GP, GS, GSw, GA, GI, GO, DX, qsb, vtb, ybf,
+    loc, sib_s, sib_r, at_s, at_r, ag_s, ag_z, ag_p, aa_s, aa_r, rs_s, rs_p, rs_z, out_l, out_s, out_r,
 ):
     dp, z = lax.axis_index("dp"), lax.axis_index("pair")
     core = lax.rem(dp, 2)
@@ -539,13 +539,15 @@
     done(sm2.at[other], sib_r.at[1])
     smb[own] = jnp.concatenate([sm2[0], sm2[1]], axis=0).astype(LOW)
 
-    exchanged = (smb, w1r, P2r, m1r, P3r, dwr, m2r)
-    gathered = (Yb, Qb, XH.at[core], dUb, dAb, dQb, sgr)
+    exchanged = (smb, w1r, None, m1r, None, dwr, m2r)
+    gathered = (Yb, Qb, XH.at[core], dUb, None, dQb)
+    summed = ((P2s, P2a, P2b, P2c), (P3s, P3a, P3b, P3c))
     passed = ((slabA.at[0], slabA.at[0]), (sm2.at[0], sm2.at[0]), (bndb.at[0], bndb.at[0]),
               (X.at[rows], X.at[rows]), (slabI.at[0], slabI.at[0]), (slabO.at[0], slabO.at[0]),
               (sn, sno), (XH.at[0], XH.at[0]))
-    written = (GO.at[0], DX.at[rows], GI.at[0], GA.at[0], GSw.at[0])
+    written = [[ref] * 3 for ref in (GO.at[0], DX.at[rows], GI.at[0], GA.at[0, 0], GSw.at[0], GA.at[0, 0])]
     state = {("pass", n): int(n < 2) for n in range(6)}
+    state["attn", 0] = 1
 
     def direct(n, src_of):
         def body(r, c):
@@ -621,33 +623,47 @@
                     def _():
                         push(slot + d, 3, own - 1)
 
+    def settle(last=True):
+        for kind, n in list(state):
+            at = state[kind, n]
+            if last and kind == "gather" and at == 0:
+                gather_forward(n)
+            if last and kind == "gather" and at < 2:
+                gather_done(n)
+            if last and kind == "sum" and at == 0:
+                sum_forward(n)
+            if last and kind == "sum" and at < 2:
+                sum_done(n)
+            if last and kind == "direct" and at == 0:
+                direct_done(n)
+            if last and kind == "pass" and at == 0:
+                pass_done(n)
+            if kind == "gather" and (last or at == 2):
+                done(gathered[n].at[pl.ds(0, 15)], ag_s.at[n])
+            elif kind == "direct" and (last or at == 1):
+                done(exchanged[n].at[pl.ds(0, 15)], aa_s.at[n])
+            elif kind == "sum" and (last or at == 2):
+                done(summed[n][1].at[pl.ds(0, 3)], rs_s.at[n, 0])
+                done(summed[n][3].at[pl.ds(0, 3)], rs_s.at[n, 1])
+            elif kind == "pass" and (last or at == 1):
+                done(passed[n][0], sib_s.at[n])
+            elif kind == "out" and last:
+                for ref, sem in zip(written[n], (out_l, out_s, out_r)):
+                    done(ref, sem.at[n])
+            elif kind == "attn":
+                for m in range(3):
+                    done(R.at[pl.ds(0, 15), m], at_s.at[m])
+                done(R.at[pl.ds(0, 7), 3], at_s.at[3])
+
+                @pl.when(jnp.logical_and(z > 0, z < 3))
+                def _():
+                    done(R.at[pl.ds(0, 16), 3], at_s.at[3])
+            else:
+                continue
+            del state[kind, n]
+
     def finish():
-        for kind, n in list(state):
-            if kind == "gather" and state[kind, n] == 0:
-                gather_forward(n)
-            if kind == "gather" and state[kind, n] == 1:
-                gather_done(n)
-            if kind == "direct" and state[kind, n] == 0:
-                direct_done(n)
-            if kind == "pass" and state[kind, n] == 0:
-                pass_done(n)
-            if kind == "gather":
-                done(gathered[n].at[pl.ds(0, 15)], ag_s.at[n])
-            if kind == "direct":
-                done(exchanged[n].at[pl.ds(0, 15)], aa_s.at[n])
-            if kind == "pass":
-                done(passed[n][0], sib_s.at[n])
-            if kind == "out":
-                done(written[n], out_l.at[n])
-                done(written[n], out_s.at[n])
-                done(written[n], out_r.at[n])
-        for m in range(3):
-            done(R.at[pl.ds(0, 15), m], at_s.at[m])
-        done(R.at[pl.ds(0, 7), 3], at_s.at[3])
-
-        @pl.when(jnp.logical_and(z > 0, z < 3))
-        def _():
-            done(R.at[pl.ds(0, 16), 3], at_s.at[3])
+        settle()
 
     def relay(m):
         def from_z(dz):
@@ -701,6 +717,8 @@
 
         from_slots(lambda s: R[s, m], write)
 
+    early_own = (0, 2, 5)
+
     def gather_start(n):
         buf = gathered[n]
         state["gather", n] = 0
@@ -709,8 +727,9 @@
             remote(buf.at[own], buf.at[own], ag_s.at[n], ag_z.at[n, z], dev(own + dz, core)).start()
 
         near(give)
-        for target in (slot_x, slot_y, slot_d):
-            remote(buf.at[own], buf.at[own], ag_s.at[n], ag_p.at[n], dev(target, core)).start()
+        if n in early_own:
+            for target in (slot_x, slot_y, slot_d):
+                remote(buf.at[own], buf.at[own], ag_s.at[n], ag_p.at[n], dev(target, core)).start()
 
     def gather_forward(n):
         buf = gathered[n]
@@ -719,14 +738,49 @@
         def pass_on(dz):
             block = buf.at[own + dz]
             done(block, ag_z.at[n, z + dz])
+            if n in early_own:
+                for target in (slot_x, slot_y, slot_d):
+                    remote(block, block, ag_s.at[n], ag_p.at[n], dev(target, core)).start()
+
+        near(pass_on)
+        if n not in early_own:
+            block = buf.at[pl.ds(line, 4)]
             for target in (slot_x, slot_y, slot_d):
                 remote(block, block, ag_s.at[n], ag_p.at[n], dev(target, core)).start()
-
-        near(pass_on)
 
     def gather_done(n):
         state["gather", n] = 2
         done(gathered[n].at[pl.ds(0, 12)], ag_p.at[n])
+
+    def sum_start(n):
+        source, plane, unused, unused = summed[n]
+        state["sum", n] = 0
+        for target in (slot_x, slot_y, slot_d):
+            remote(
+                source.at[pl.ds(target - z, 4)], plane.at[line // 4],
+                rs_s.at[n, 0], rs_p.at[n], dev(target, core),
+            ).start()
+        plane[line // 4] = source[pl.ds(line, 4)]
+
+    def sum_forward(n):
+        unused, plane, along, final = summed[n]
+        state["sum", n] = 1
+        done(plane.at[pl.ds(0, 3)], rs_p.at[n])
+        along[...] = jnp.sum(plane[...].astype(F32), axis=0).astype(LOW)
+
+        def give(dz):
+            remote(
+                along.at[z + dz], final.at[z], rs_s.at[n, 1], rs_z.at[n], dev(own + dz, core)
+            ).start()
+
+        near(give)
+        final[z] = along[z]
+
+    def sum_done(n):
+        final = summed[n][3]
+        state["sum", n] = 2
+        done(final.at[pl.ds(0, 3)], rs_z.at[n])
+        return jnp.sum(final[...].astype(F32), axis=0)
 
     def prepare_ffn():
         row = lax.broadcasted_iota(jnp.int32, (384, 512), 0)
@@ -784,10 +838,9 @@
     arrive(0)
     queries = (dot_nn(cls_low, WN[0]) + vec(0)).astype(LOW)
     Qb[own] = queries
+    gather_start(1)
     relay(2)
     hop(2)
-    direct(1, lambda t: w1s_.at[t])
-    gather_start(1)
     arrive(1)
     qsb[...] = (dot_nt(expand_heads(queries), WN[1]) * (HD**-0.5)).astype(LOW)
     ST[...] = dot_nt(qsb[...], X[...])
@@ -801,7 +854,7 @@
         Pb[at, :] = p.astype(LOW)
         return c
 
-    lax.fori_loop(0, 12, soften, 0)
+    lax.fori_loop(0, 12, soften, 0, unroll=4)
     ybf[...] = dot_nn(Pb[...], X[...]).astype(LOW)
     arrive(2)
     mixed = (pick_heads(dot_nn(ybf[...], WN[2])) + vec(6)).astype(LOW)
@@ -814,6 +867,7 @@
     normed = hat_one * vec(18) + vec(24)
     Yb[own] = normed.astype(LOW)
     gather_start(0)
+    direct(1, lambda t: w1s_.at[t])
 
     early = jnp.concatenate(
         [ybf[...].astype(F32), cls_in, mixed.astype(F32), jnp.zeros((32, 768), F32)], axis=0
@@ -849,11 +903,11 @@
     hidden, unused = gelu_parts(act)
     Gb[...] = hidden.astype(LOW)
     P2s[...] = dot_nn(Gb[...], W2[...]).astype(LOW).reshape(16, 16, 768)
-    direct(2, lambda t: P2s.at[t])
-    P2r[own] = P2s[own]
-    gather_forward(1)
-    direct_done(2)
-    second = normed + jnp.sum(P2r[...].astype(F32), axis=0) + vec(54)
+    sum_start(0)
+    direct(3, lambda t: m1s.at[t])
+    sum_forward(0)
+    hidden_sum = sum_done(0)
+    second = normed + hidden_sum + vec(54)
     centred = second - jnp.mean(second, axis=1, keepdims=True)
     rstd_two = lax.rsqrt(jnp.mean(centred * centred, axis=1, keepdims=True) + NORM_EPS)
     hat_two = centred * rstd_two
@@ -867,7 +921,7 @@
     XH[core, own] = jnp.concatenate([hat_two, extra], axis=1).astype(LOW)
     gather_start(2)
     gather_forward(2)
-    direct(3, lambda t: m1s.at[t])
+    gather_forward(1)
     gather_done(2)
     remote(XH.at[core], XH.at[core], sib_s.at[7], sib_r.at[7], sibling).start()
     state["pass", 7] = 0
@@ -920,8 +974,7 @@
     unused, slope = gelu_parts(Act[...])
     da = (dot_nt(dZb[...], W2[...]) * slope).astype(LOW)
     P3s[...] = dot_nt(da, W1[...]).astype(LOW).reshape(16, 16, 768)
-    direct(4, lambda t: P3s.at[t])
-    P3r[own] = P3s[own]
+    sum_start(1)
     DX[0:768, 0:256] = dot_tn(all_y, da)
 
     def write_dw(slot, v):
@@ -929,6 +982,7 @@
 
     to_slots(lambda w: DX[w, 0:256], write_dw)
     direct(5, lambda t: dws.at[t])
+    sum_forward(1)
     dwr[own] = dws[own]
     db1 = jnp.sum(da.astype(F32), axis=0, keepdims=True)
     dw2 = dot_tn(Gb[...], dZb[...])
@@ -938,9 +992,9 @@
     remote(GO.at[other], go_ref.at[core], out_s.at[0], out_r.at[0], sibling).start()
     state["out", 0] = 0
     own_rows = pl.ds(pl.multiple_of(16 * own, 16), 16)
-    direct_done(4)
-
-    grad_normed = Dout[own_rows, :] + jnp.sum(P3r[...].astype(F32), axis=0)
+    normed_sum = sum_done(1)
+
+    grad_normed = Dout[own_rows, :] + normed_sum
     inner = grad_normed * vec(18)
     grad_one = rstd_one * (
         inner - jnp.mean(inner, axis=1, keepdims=True)
@@ -948,25 +1002,19 @@
     )
     grad_lift = grad_one.astype(LOW)
     grad_mixed = dot_nt(grad_lift, WN[3]).astype(LOW)
-    dUb[own] = grad_lift
-    dAb[own] = grad_mixed
-    gather_start(3)
-    gather_start(4)
     dg1 = jnp.sum(grad_normed * hat_one, axis=0, keepdims=True)
     ds1 = jnp.sum(grad_normed, axis=0, keepdims=True)
-    sgr[own] = jnp.concatenate(
+    partial_sums = jnp.concatenate(
         [dg1[:, 128 * i : 128 * i + 128] for i in range(6)]
         + [ds1[:, 128 * i : 128 * i + 128] for i in range(6)]
         + [db1[:, 0:128], db1[:, 128:256], jnp.zeros((2, 128), F32)], axis=0,
     )
-    gather_start(6)
+    dUb[own] = jnp.concatenate([grad_one, partial_sums], axis=1).astype(LOW)
+    gather_start(3)
     spread = expand_heads(grad_mixed)
     vtb[...] = dot_nt(spread, WN[2]).astype(LOW)
     constant = jnp.sum(spread.astype(F32) * vec(6), axis=1, keepdims=True)
     ST[...] = dot_nt(vtb[...], X[...]) + constant
-    gather_forward(3)
-    gather_forward(4)
-    gather_forward(6)
 
     def harden(h, c):
         at = pl.ds(pl.multiple_of(16 * h, 16), 16)
@@ -975,8 +1023,11 @@
         DSb[at, :] = (p * (dprob - total)).astype(LOW)
         return c
 
-    lax.fori_loop(0, 12, harden, 0)
+    lax.fori_loop(0, 12, harden, 0, unroll=4)
     late = (dot_nn(DSb[...], X[...]) * (HD**-0.5)).astype(LOW)
+    grad_query = pick_heads(dot_nn(late, WN[1])).astype(LOW)
+    dQb[own] = grad_query
+    gather_start(5)
     DX[0:768, 0:256] = jnp.concatenate(
         [late.astype(F32), jnp.zeros((64, 768), F32)], axis=0
     ).T
@@ -987,9 +1038,7 @@
     to_slots(lambda w: DX[w, 0:256], write_m2)
     direct(6, lambda t: m2s.at[t])
     m2r[own] = m2s[own]
-    grad_query = pick_heads(dot_nn(late, WN[1])).astype(LOW)
-    dQb[own] = grad_query
-    gather_start(5)
+    gather_forward(3)
 
     grad_cls = grad_one + dot_nt(grad_query, WN[0])
     cls_high, cls_rest = split_low(grad_cls)
@@ -1026,8 +1075,14 @@
     state["out", 2] = 0
 
     def put(m, v):
-        GA[0, :, 768 * m : 768 * m + 768] = v[0:24]
-        GA[1, :, 768 * m : 768 * m + 768] = v[24:48]
+        GA[m // 2, 0, :, 768 * (m % 2) : 768 * (m % 2) + 768] = v[0:24]
+        GA[m // 2, 1, :, 768 * (m % 2) : 768 * (m % 2) + 768] = v[24:48]
+
+    def hand_out(half, n):
+        part = ga_ref.at[core, :, pl.ds(1536 * half, 1536)]
+        pltpu.make_async_copy(GA.at[half, core], part, out_l.at[n]).start()
+        remote(GA.at[half, other], part, out_s.at[n], out_r.at[n], sibling).start()
+        state["out", n] = 0
 
     def factor_sum(messages, columns):
         def body(s, total):
@@ -1036,64 +1091,68 @@
             )
             return total + dot_nn(messages[s], wide)
 
-        return lax.fori_loop(0, 16, body, jnp.zeros((48, 768), F32))
-
-    gather_done(1)
-    gather_done(4)
-    direct_done(3)
-    put(2, factor_sum(m1r, dAb))
-    gather_done(3)
+        return lax.fori_loop(0, 16, body, jnp.zeros((48, 768), F32), unroll=4)
 
     def columns_of(at):
         return jnp.concatenate(
             [m1r[s, :, at : at + 16].astype(F32) for s in range(16)], axis=1
         ).astype(LOW)
 
-    all_du = dUb[...].reshape(256, 768)
+    gather_done(3)
+    all_du = dUb[...].reshape(256, 896)[:, 0:768]
+    all_da = dot_nt(all_du, WN[3]).astype(LOW)
+    dAb[...] = all_da.reshape(16, 16, 768)
+    direct_done(3)
+    put(2, factor_sum(m1r, dAb))
     put(3, dot_nn(columns_of(208), all_du))
-    direct_done(6)
-    put(1, factor_sum(m2r, Qb))
-    gather_done(5)
-    all_dq = dQb[...].reshape(256, 768)
-    put(0, dot_nn(columns_of(192), all_dq))
-    pltpu.make_async_copy(GA.at[core], ga_ref.at[core], out_l.at[3]).start()
-    remote(GA.at[other], ga_ref.at[core], out_s.at[3], out_r.at[3], sibling).start()
-    state["out", 3] = 0
-
-    gather_done(6)
-    sums = jnp.sum(sgr[...], axis=0)
+    hand_out(1, 5)
+    cls_columns = columns_of(192)
+
+    parts = [dUb[i, :, 768:896].astype(F32) for i in range(16)]
+    sums = parts[0]
+    for part in parts[1:]:
+        sums = sums + part
     hidden_rows = []
     for g in range(8):
-        wide = jnp.concatenate(
-            [sgr[4 * (g // 2) + i, 12 + g % 2 : 13 + g % 2, :] for i in range(4)], axis=1
+        hidden_rows.append(
+            jnp.concatenate(
+                [parts[4 * (g // 2) + i][12 + g % 2 : 13 + g % 2] for i in range(4)], axis=1
+            )
         )
-        hidden_rows.append(wide)
     wide = jnp.concatenate(hidden_rows, axis=0)
-    high, rest = split_low(wide)
-    rest, last = split_low(wide - high.astype(F32))
-    narrow = dot_nt(high, Emat[...]) + dot_nt(rest, Emat[...]) + dot_nt(last, Emat[...])
+    narrow = dot_nt(wide.astype(LOW), Emat[...])
 
     def six(v):
         return [v[:, 128 * i : 128 * i + 128] for i in range(6)]
 
-    lines = six(jnp.sum(all_dq.astype(F32), axis=0, keepdims=True))
-    lines += six(jnp.sum(dAb[...].reshape(256, 768).astype(F32), axis=0, keepdims=True))
+    lines = six(jnp.sum(all_da.astype(F32), axis=0, keepdims=True))
     lines += six(jnp.sum(all_du.astype(F32), axis=0, keepdims=True))
     lines += [sums[0:12]]
     for g in range(8):
         lines += [narrow[g : g + 1, 128 * i : 128 * i + 128] for i in range(3)]
     lines += six(db2) + six(dg2) + six(ds2) + [jnp.zeros((8, 128), F32)]
-    packed = jnp.concatenate(lines, axis=0)
+    GP[6:80] = jnp.concatenate(lines, axis=0)
     for g in range(8):
         for i in range(4):
             at = 9 * g + 9 * i // 4
-            GS[g, i] = packed[at : at + 8]
+            if at > 5:
+                GS[g, i] = GP[at : at + 8]
+    gather_done(1)
+    settle(False)
+    direct_done(6)
+    put(1, factor_sum(m2r, Qb))
+    gather_done(5)
+    all_dq = dQb[...].reshape(256, 768)
+    put(0, dot_nn(cls_columns, all_dq))
+    hand_out(0, 3)
+    GP[0:6] = jnp.concatenate(six(jnp.sum(all_dq.astype(F32), axis=0, keepdims=True)), axis=0)
+    for i in range(3):
+        GS[0, i] = GP[9 * i // 4 : 9 * i // 4 + 8]
     for k in range(2):
         GSw[k] = GS[gy + k, z]
     pltpu.make_async_copy(GSw.at[core], gs_ref.at[core], out_l.at[4]).start()
     remote(GSw.at[other], gs_ref.at[core], out_s.at[4], out_r.at[4], sibling).start()
     state["out", 4] = 0
-
     finish()
 
 
@@ -1110,17 +1169,20 @@
         V((192, 1024), F32), V((192, 1024), LOW), V((192, 1024), LOW), V((384, 512), LOW),
         V((8, 8, 512), F32),
         V((16, 48, 256), LOW), V((16, 48, 256), LOW), V((768, 256), LOW), V((256, 768), LOW),
-        V((16, 16, 768), LOW), V((16, 16, 768), LOW), V((16, 16, 768), LOW),
+        V((16, 16, 768), LOW), V((16, 16, 768), LOW), V((4, 4, 16, 768), LOW),
+        V((4, 16, 768), LOW), V((4, 16, 768), LOW),
         V((2, 16, 16, 896), LOW), V((256, 768), F32), V((256, 768), LOW), V((256, 256), LOW),
-        V((256, 256), F32), V((16, 16, 768), LOW), V((16, 16, 768), LOW), V((16, 16, 768), LOW),
-        V((16, 16, 768), LOW), V((16, 16, 768), LOW), V((16, 16, 768), LOW),
+        V((256, 256), F32), V((16, 16, 768), LOW), V((4, 4, 16, 768), LOW),
+        V((4, 16, 768), LOW), V((4, 16, 768), LOW), V((16, 16, 768), LOW),
+        V((16, 16, 768), LOW), V((16, 16, 896), LOW), V((16, 16, 768), LOW),
         V((16, 48, 256), LOW), V((16, 48, 256), LOW), V((16, 48, 256), LOW), V((16, 48, 256), LOW),
-        V((16, 48, 256), LOW), V((16, 48, 256), LOW), V((16, 16, 128), F32),
-        V((8, 4, 8, 128), F32), V((2, 8, 128), F32), V((2, 24, 3072), F32), V((2, 24, 3072), F32),
+        V((16, 48, 256), LOW), V((16, 48, 256), LOW),
+        V((80, 128), F32), V((8, 4, 8, 128), F32), V((2, 8, 128), F32), V((2, 2, 24, 1536), F32), V((2, 24, 3072), F32),
         V((2, 96, 768), F32), V((1024, 768), F32), V((192, 768), LOW), V((192, 768), LOW),
         V((192, 768), LOW),
         dma((4,)), dma((8,)), dma((8,)), dma((4,)), dma((16, 4, 2)), dma((7,)), dma((7, 4)),
-        dma((7,)), dma((7,)), dma((7,)), dma((5,)), dma((5,)), dma((5,)),
+        dma((7,)), dma((7,)), dma((7,)), dma((2, 2)), dma((2,)), dma((2,)),
+        dma((6,)), dma((6,)), dma((6,)),
     ]
     shapes = (
         (2, 24, 3072), (2, 24, 3072), (2, 96, 768), (2, 8, 128), (512, 768), (512, 768)
@@ -1166,18 +1228,18 @@
 
 
 def update_call(attn, inner, outer, small, grad_question, grad_passage):
-    wide = pl.BlockSpec((1, 24, 768), lambda i: (i // 4, 0, i % 4))
-    tall = pl.BlockSpec((1, 24, 768), lambda i: (i // 4, i % 4, 0))
+    wide = pl.BlockSpec((1, 24, 3072), lambda i: (i, 0, 0))
+    tall = pl.BlockSpec((1, 96, 768), lambda i: (i, 0, 0))
     vector = pl.BlockSpec((2, 288), lambda i: (0, 0))
     window = pl.BlockSpec((2, 8, 128), lambda i: (0, 0, 0))
-    token = pl.BlockSpec((64, 768), lambda i: (i, 0))
+    token = pl.BlockSpec((256, 768), lambda i: (i, 0))
 
     def like(a):
         return jax.ShapeDtypeStruct(a.shape, F32)
 
     return pl.pallas_call(
         update_kernel,
-        grid=(8,),
+        grid=(2,),
         out_shape=[like(g[0]) for g in (attn, inner, outer, small) for _ in range(3)]
         + [like(grad_question), like(grad_passage)],
         in_specs=[wide] * 8 + [tall] * 4 + [vector] * 3 + [window, token, token],

time: 148 us -> 133 us (0.90)
  Pallas kernels: 147 us -> 132 us
    pallas_call x1, Pallas kernels: 136 us -> 125 us  [kernel_call(): pl.pallas_call(step_kernel, out_shape=[jax.ShapeDtypeStruct(s, F32) for s...]
    pallas_call x1, Pallas kernels: 10.5 us -> 7.22 us  [update_call(): pl.pallas_call(update_kernel, grid=(2,), out_shape=[like(g[0]) for g in (...]
where the time goes in v3:
time: 133 us
  Pallas kernels  132 us (99%)
    pallas_call x1, Pallas kernels, kernel_call(): pl.pallas_call(step_kernel, out_shape=[jax.ShapeDtypeStruct(s, F32) for s...  125 us
    pallas_call x1, Pallas kernels, update_call(): pl.pallas_call(update_kernel, grid=(2,), out_shape=[like(g[0]) for g in (...  7.22 us

profile of v3, /device:TPU:0, one launch (start us, length us, event | category | flops | bytes accessed | tf_op | source)
XLA Modules:
  0.0 132.6 jit_solution(4982881269879738279)
XLA Ops:
  0.6 124.6 %shard_map.263 = (f32[2,24,3072]{2,1,0:T(8,128)}, f32[2,24,3072]{2,1,0:T(8,128)}, f32[2,96,768]{2,1,0:T(8,128)}, f32[2,8,128]{2,1,0:T(8,128)}, f32[512,768]{1,0:T(8,128)}, /*index=5*/f32[512,768]{1,0:T(8,128)}) custom-call(bf16[512,768]{1,0:T(8,128)(2,1)} %bitcast.5, bf16[512,768]{1,0:T(8,128)(2,1)} %bitcast.6, f32[2,24,3072]{2,1,0:T(8,128)} %refs_0_.1, ...), custom_call_target="tpu_custom_call" | custom-call | tf_op jit(solution)/shard_map/pallas_call | solution.py:1190
  125.2 7.2 %shard_map.264 = (f32[2,24,3072]{2,1,0:T(8,128)}, f32[2,24,3072]{2,1,0:T(8,128)}, f32[2,24,3072]{2,1,0:T(8,128)}, f32[2,24,3072]{2,1,0:T(8,128)}, f32[2,24,3072]...) custom-call(f32[2,24,3072]{2,1,0:T(8,128)} %refs_0_.1, ...), custom_call_target="tpu_custom_call" | custom-call | tf_op jit(solution)/shard_map/pallas_call | solution.py:1240

commit v4 on v3

--- a/solution.py
+++ b/solution.py
@@ -665,25 +665,26 @@
     def finish():
         settle()
 
-    def relay(m):
-        def from_z(dz):
+    def relay_z(m):
+        def give(dz):
             got(own + dz, m)
             for target in (slot_x, slot_y):
                 push(own + dz, m, target)
 
-        near(from_z)
-
-        def from_plane(dz):
+        near(give)
+
+    def relay_plane(m):
+        def give(dz):
             for slot, target, half in ((slot_x + dz, slot_y, 0), (slot_y + dz, slot_x, 1)):
                 got(slot, m)
                 part = R.at[slot, m, :, pl.ds(384 * half, 384)]
                 remote(part, part, at_s.at[m], at_r.at[slot, m, half], dev(target, core)).start()
 
-        near(from_plane, 0)
+        near(give, 0)
 
     def from_slots(read, write):
         def body(g, c):
-            got = [read(4 * g + i).astype(F32) for i in range(4)]
+            got = [read(4 * g + i) for i in range(4)]
             natural = jnp.concatenate([v[0:24] for v in got] + [v[24:48] for v in got], axis=0)
             write(pl.ds(pl.multiple_of(192 * g, 64), 192), natural.astype(LOW))
             return c
@@ -697,10 +698,19 @@
                 part = jnp.concatenate(
                     [v[24 * i : 24 * i + 24], v[96 + 24 * i : 96 + 24 * i + 24]], axis=0
                 )
-                write(4 * g + i, part.astype(LOW))
+                write(4 * g + i, part)
             return c
 
         lax.fori_loop(0, 4, body, 0)
+
+    def pack(v):
+        tail = jnp.concatenate([v[0:24, 128:192], v[24:48, 128:192]], axis=1)
+        return jnp.concatenate([v[:, 0:128], tail, jnp.zeros((8, 128), F32)], axis=0).astype(LOW)
+
+    def unpack(packed):
+        v = packed.astype(F32)
+        tail = jnp.concatenate([v[48:72, 0:64], v[48:72, 64:128]], axis=0)
+        return jnp.concatenate([v[0:48], tail], axis=1)
 
     def arrive(m):
         def body(zz, c):
@@ -715,9 +725,9 @@
         def write(where, v):
             WN[m, where, :] = v
 
-        from_slots(lambda s: R[s, m], write)
-
-    early_own = (0, 2, 5)
+        from_slots(lambda s: R[s, m].astype(F32), write)
+
+    early_own = (0, 2)
 
     def gather_start(n):
         buf = gathered[n]
@@ -788,19 +798,19 @@
         Emat[...] = jnp.where(col == 128 * (row // 96) + lax.rem(row, 96), 1.0, 0.0).astype(LOW)
         done(slabI.at[core], loc.at[2])
         pass_done(4)
-        for g in range(8):
-            cols = slice(384 * g, 384 * g + 384)
-            part = jnp.concatenate([slabI[0, :, cols], slabI[1, :, cols]], axis=0).astype(LOW)
-            wide = dot_nn(part, Emat[...]).astype(LOW)
+        for g in range(4):
+            halves = []
+            for k in range(2):
+                cols = slice(768 * g + 384 * k, 768 * g + 384 * k + 384)
+                halves.append(jnp.concatenate([slabI[0, :, cols], slabI[1, :, cols]], axis=0))
             for i in range(4):
-                w1s_[4 * (g // 2) + i, :, 128 * (g % 2) : 128 * (g % 2) + 128] = wide[
-                    :, 128 * i : 128 * i + 128
-                ]
+                lanes = slice(96 * i, 96 * i + 96)
+                w1s_[4 * g + i] = pack(jnp.concatenate([half[:, lanes] for half in halves], axis=1))
         w1r[own] = w1s_[own]
         done(slabO.at[core], loc.at[3])
         pass_done(5)
-        gap = jnp.zeros((32, 768), F32)
-        W2[...] = jnp.concatenate([slabO[0], gap, slabO[1], gap], axis=0).astype(LOW)
+        gap = jnp.zeros((64, 768), F32)
+        W2[...] = jnp.concatenate([slabO[0], slabO[1], gap], axis=0).astype(LOW)
 
     def natural_small():
         direct_done(0)
@@ -819,7 +829,7 @@
     def vec(row, count=6, ref=sn):
         return jnp.concatenate([ref[row + i : row + i + 1, :] for i in range(count)], axis=1)
 
-    relay(0)
+    relay_z(0)
     hop(0)
     pass_done(2)
     done(X.at[pl.ds(0, 512)], loc.at[1])
@@ -831,16 +841,19 @@
     first = jnp.where(token == starts, 1.0, 0.0).astype(LOW)
     cls_in = dot_nn(first, X[...])
     cls_low = cls_in.astype(LOW)
+    relay_z(1)
+    relay_plane(0)
     natural_small()
     prepare_ffn()
-    relay(1)
     hop(1)
+    relay_z(2)
+    relay_plane(1)
     arrive(0)
     queries = (dot_nn(cls_low, WN[0]) + vec(0)).astype(LOW)
     Qb[own] = queries
     gather_start(1)
-    relay(2)
     hop(2)
+    relay_plane(2)
     arrive(1)
     qsb[...] = (dot_nt(expand_heads(queries), WN[1]) * (HD**-0.5)).astype(LOW)
     ST[...] = dot_nt(qsb[...], X[...])
@@ -875,7 +888,7 @@
     DX[0:768, 0:256] = early.T
 
     def write_m1(slot, v):
-        m1s[slot] = v
+        m1s[slot] = v.astype(LOW)
 
     to_slots(lambda w: DX[w, 0:256], write_m1)
     m1r[own] = m1s[own]
@@ -888,14 +901,18 @@
     group = pl.multiple_of(128 * z, 128)
     gy = 4 * y + 2 * x
     b1_row = jnp.concatenate(
-        [b1p[gy, 0:1, pl.ds(group, 128)], b1p[gy + 1, 0:1, pl.ds(group, 128)]], axis=1
+        [
+            b1p[gy, 0:1, pl.ds(group, 128)][:, 0:96], b1p[gy + 1, 0:1, pl.ds(group, 128)][:, 0:96],
+            jnp.zeros((1, 64), F32),
+        ], axis=1,
     )
     direct_done(1)
 
     def write_w1(where, v):
         W1[where, :] = v
 
-    from_slots(lambda s: w1r[s], write_w1)
+    pad = jnp.zeros((48, 64), F32)
+    from_slots(lambda s: jnp.concatenate([unpack(w1r[s]), pad], axis=1), write_w1)
     gather_done(0)
     all_y = Yb[...].reshape(256, 768)
     act = dot_nn(all_y, W1[...]) + b1_row
@@ -978,7 +995,7 @@
     DX[0:768, 0:256] = dot_tn(all_y, da)
 
     def write_dw(slot, v):
-        dws[slot] = v
+        dws[slot] = pack(v)
 
     to_slots(lambda w: DX[w, 0:256], write_dw)
     direct(5, lambda t: dws.at[t])
@@ -987,7 +1004,7 @@
     db1 = jnp.sum(da.astype(F32), axis=0, keepdims=True)
     dw2 = dot_tn(Gb[...], dZb[...])
     GO[0] = dw2[0:96]
-    GO[1] = dw2[128:224]
+    GO[1] = dw2[96:192]
     pltpu.make_async_copy(GO.at[core], go_ref.at[core], out_l.at[0]).start()
     remote(GO.at[other], go_ref.at[core], out_s.at[0], out_r.at[0], sibling).start()
     state["out", 0] = 0
@@ -1033,7 +1050,7 @@
     ).T
 
     def write_m2(slot, v):
-        m2s[slot] = v
+        m2s[slot] = pack(v)
 
     to_slots(lambda w: DX[w, 0:256], write_m2)
     direct(6, lambda t: m2s.at[t])
@@ -1063,13 +1080,13 @@
     state["out", 1] = 0
 
     direct_done(5)
-    for g in range(8):
-        wide = jnp.concatenate(
-            [dwr[4 * (g // 2) + i, :, 128 * (g % 2) : 128 * (g % 2) + 128] for i in range(4)], axis=1
-        )
-        narrow = dot_nt(wide, Emat[...])
-        GI[0, :, 384 * g : 384 * g + 384] = narrow[0:24]
-        GI[1, :, 384 * g : 384 * g + 384] = narrow[24:48]
+    for g in range(4):
+        parts = [unpack(dwr[4 * g + i]) for i in range(4)]
+        for k in range(2):
+            block = jnp.concatenate([v[:, 96 * k : 96 * k + 96] for v in parts], axis=1)
+            cols = slice(768 * g + 384 * k, 768 * g + 384 * k + 384)
+            GI[0, :, cols] = block[0:24]
+            GI[1, :, cols] = block[24:48]
     pltpu.make_async_copy(GI.at[core], gi_ref.at[core], out_l.at[2]).start()
     remote(GI.at[other], gi_ref.at[core], out_s.at[2], out_r.at[2], sibling).start()
     state["out", 2] = 0
@@ -1084,12 +1101,9 @@
         remote(GA.at[half, other], part, out_s.at[n], out_r.at[n], sibling).start()
         state["out", n] = 0
 
-    def factor_sum(messages, columns):
+    def factor_sum(read, columns):
         def body(s, total):
-            wide = jnp.concatenate(
-                [expand_heads(columns[s]), jnp.zeros((64, 768), LOW)], axis=0
-            )
-            return total + dot_nn(messages[s], wide)
+            return total + dot_nn(read(s), expand_heads(columns[s]))
 
         return lax.fori_loop(0, 16, body, jnp.zeros((48, 768), F32), unroll=4)
 
@@ -1103,7 +1117,7 @@
     all_da = dot_nt(all_du, WN[3]).astype(LOW)
     dAb[...] = all_da.reshape(16, 16, 768)
     direct_done(3)
-    put(2, factor_sum(m1r, dAb))
+    put(2, factor_sum(lambda s: m1r[s, :, 0:192], dAb))
     put(3, dot_nn(columns_of(208), all_du))
     hand_out(1, 5)
     cls_columns = columns_of(192)
@@ -1112,15 +1126,15 @@
     sums = parts[0]
     for part in parts[1:]:
         sums = sums + part
-    hidden_rows = []
-    for g in range(8):
-        hidden_rows.append(
+    wide = [jnp.concatenate([part[12:13], part[13:14]], axis=1) for part in parts]
+    narrow = jnp.concatenate(
+        [
             jnp.concatenate(
-                [parts[4 * (g // 2) + i][12 + g % 2 : 13 + g % 2] for i in range(4)], axis=1
+                [wide[4 * (g // 2) + i][:, 96 * (g % 2) : 96 * (g % 2) + 96] for i in range(4)], axis=1
             )
-        )
-    wide = jnp.concatenate(hidden_rows, axis=0)
-    narrow = dot_nt(wide.astype(LOW), Emat[...])
+            for g in range(8)
+        ], axis=0,
+    )
 
     def six(v):
         return [v[:, 128 * i : 128 * i + 128] for i in range(6)]
@@ -1140,7 +1154,7 @@
     gather_done(1)
     settle(False)
     direct_done(6)
-    put(1, factor_sum(m2r, Qb))
+    put(1, factor_sum(lambda s: unpack(m2r[s]).astype(LOW), Qb))
     gather_done(5)
     all_dq = dQb[...].reshape(256, 768)
     put(0, dot_nn(cls_columns, all_dq))
@@ -1168,15 +1182,15 @@
         V((4, 768, 768), LOW), V((72, 128), F32), V((72, 128), F32), V((192, 1024), F32),
         V((192, 1024), F32), V((192, 1024), LOW), V((192, 1024), LOW), V((384, 512), LOW),
         V((8, 8, 512), F32),
-        V((16, 48, 256), LOW), V((16, 48, 256), LOW), V((768, 256), LOW), V((256, 768), LOW),
+        V((16, 80, 128), LOW), V((16, 80, 128), LOW), V((768, 256), LOW), V((256, 768), LOW),
         V((16, 16, 768), LOW), V((16, 16, 768), LOW), V((4, 4, 16, 768), LOW),
         V((4, 16, 768), LOW), V((4, 16, 768), LOW),
         V((2, 16, 16, 896), LOW), V((256, 768), F32), V((256, 768), LOW), V((256, 256), LOW),
         V((256, 256), F32), V((16, 16, 768), LOW), V((4, 4, 16, 768), LOW),
         V((4, 16, 768), LOW), V((4, 16, 768), LOW), V((16, 16, 768), LOW),
         V((16, 16, 768), LOW), V((16, 16, 896), LOW), V((16, 16, 768), LOW),
-        V((16, 48, 256), LOW), V((16, 48, 256), LOW), V((16, 48, 256), LOW), V((16, 48, 256), LOW),
-        V((16, 48, 256), LOW), V((16, 48, 256), LOW),
+        V((16, 48, 256), LOW), V((16, 48, 256), LOW), V((16, 80, 128), LOW), V((16, 80, 128), LOW),
+        V((16, 80, 128), LOW), V((16, 80, 128), LOW),
         V((80, 128), F32), V((8, 4, 8, 128), F32), V((2, 8, 128), F32), V((2, 2, 24, 1536), F32), V((2, 24, 3072), F32),
         V((2, 96, 768), F32), V((1024, 768), F32), V((192, 768), LOW), V((192, 768), LOW),
         V((192, 768), LOW),

time: 133 us -> 131 us (0.985)
  Pallas kernels: 132 us -> 130 us
    pallas_call x1, Pallas kernels: 125 us -> 123 us  [kernel_call(): pl.pallas_call(step_kernel, out_shape=[jax.ShapeDtypeStruct(s, F32) for s...]
where the time goes in v4:
time: 131 us
  Pallas kernels  130 us (99%)
    pallas_call x1, Pallas kernels, kernel_call(): pl.pallas_call(step_kernel, out_shape=[jax.ShapeDtypeStruct(s, F32) for s...  123 us
    pallas_call x1, Pallas kernels, update_call(): pl.pallas_call(update_kernel, grid=(2,), out_shape=[like(g[0]) for g in (...  7.22 us

profile of v4, /device:TPU:0, one launch (start us, length us, event | category | flops | bytes accessed | tf_op | source)
XLA Modules:
  0.0 130.7 jit_solution(10152048146787751999)
XLA Ops:
  0.6 122.7 %shard_map.263 = (f32[2,24,3072]{2,1,0:T(8,128)}, f32[2,24,3072]{2,1,0:T(8,128)}, f32[2,96,768]{2,1,0:T(8,128)}, f32[2,8,128]{2,1,0:T(8,128)}, f32[512,768]{1,0:T(8,128)}, /*index=5*/f32[512,768]{1,0:T(8,128)}) custom-call(bf16[512,768]{1,0:T(8,128)(2,1)} %bitcast.5, bf16[512,768]{1,0:T(8,128)(2,1)} %bitcast.6, f32[2,24,3072]{2,1,0:T(8,128)} %refs_0_.1, ...), custom_call_target="tpu_custom_call" | custom-call | tf_op jit(solution)/shard_map/pallas_call | solution.py:1204
  123.3 7.2 %shard_map.264 = (f32[2,24,3072]{2,1,0:T(8,128)}, f32[2,24,3072]{2,1,0:T(8,128)}, f32[2,24,3072]{2,1,0:T(8,128)}, f32[2,24,3072]{2,1,0:T(8,128)}, f32[2,24,3072]...) custom-call(f32[2,24,3072]{2,1,0:T(8,128)} %refs_0_.1, ...), custom_call_target="tpu_custom_call" | custom-call | tf_op jit(solution)/shard_map/pallas_call | solution.py:1254

commit v5 on v4

--- a/solution.py
+++ b/solution.py
@@ -727,7 +727,7 @@
 
         from_slots(lambda s: R[s, m].astype(F32), write)
 
-    early_own = (0, 2)
+    early_own = (0, 2, 3)
 
     def gather_start(n):
         buf = gathered[n]
@@ -762,29 +762,43 @@
         state["gather", n] = 2
         done(gathered[n].at[pl.ds(0, 12)], ag_p.at[n])
 
+    def each_z(f):
+        for d in range(3, -1, -1):
+            for dz in (d, -d) if d else (0,):
+                @pl.when(jnp.logical_and(z + dz >= 0, z + dz <= 3))
+                def _():
+                    f(dz)
+
     def sum_start(n):
         source, plane, unused, unused = summed[n]
         state["sum", n] = 0
-        for target in (slot_x, slot_y, slot_d):
-            remote(
-                source.at[pl.ds(target - z, 4)], plane.at[line // 4],
-                rs_s.at[n, 0], rs_p.at[n], dev(target, core),
-            ).start()
+
+        def give(dz):
+            for target in (slot_x, slot_y, slot_d):
+                remote(
+                    source.at[target + dz], plane.at[line // 4, z + dz],
+                    rs_s.at[n, 0], rs_p.at[n, z + dz], dev(target, core),
+                ).start()
+
+        each_z(give)
         plane[line // 4] = source[pl.ds(line, 4)]
 
     def sum_forward(n):
         unused, plane, along, final = summed[n]
         state["sum", n] = 1
-        done(plane.at[pl.ds(0, 3)], rs_p.at[n])
-        along[...] = jnp.sum(plane[...].astype(F32), axis=0).astype(LOW)
 
         def give(dz):
-            remote(
-                along.at[z + dz], final.at[z], rs_s.at[n, 1], rs_z.at[n], dev(own + dz, core)
-            ).start()
-
-        near(give)
-        final[z] = along[z]
+            done(plane.at[pl.ds(0, 3), z + dz], rs_p.at[n, z + dz])
+            total = jnp.sum(plane[:, z + dz].astype(F32), axis=0).astype(LOW)
+            if dz == 0:
+                final[z] = total
+            else:
+                along[z + dz] = total
+                remote(
+                    along.at[z + dz], final.at[z], rs_s.at[n, 1], rs_z.at[n], dev(own + dz, core)
+                ).start()
+
+        each_z(give)
 
     def sum_done(n):
         final = summed[n][3]
@@ -867,7 +881,7 @@
         Pb[at, :] = p.astype(LOW)
         return c
 
-    lax.fori_loop(0, 12, soften, 0, unroll=4)
+    lax.fori_loop(0, 12, soften, 0, unroll=12)
     ybf[...] = dot_nn(Pb[...], X[...]).astype(LOW)
     arrive(2)
     mixed = (pick_heads(dot_nn(ybf[...], WN[2])) + vec(6)).astype(LOW)
@@ -1040,7 +1054,7 @@
         DSb[at, :] = (p * (dprob - total)).astype(LOW)
         return c
 
-    lax.fori_loop(0, 12, harden, 0, unroll=4)
+    lax.fori_loop(0, 12, harden, 0, unroll=12)
     late = (dot_nn(DSb[...], X[...]) * (HD**-0.5)).astype(LOW)
     grad_query = pick_heads(dot_nn(late, WN[1])).astype(LOW)
     dQb[own] = grad_query
@@ -1105,7 +1119,7 @@
         def body(s, total):
             return total + dot_nn(read(s), expand_heads(columns[s]))
 
-        return lax.fori_loop(0, 16, body, jnp.zeros((48, 768), F32), unroll=4)
+        return lax.fori_loop(0, 16, body, jnp.zeros((48, 768), F32), unroll=16)
 
     def columns_of(at):
         return jnp.concatenate(
@@ -1195,7 +1209,7 @@
         V((2, 96, 768), F32), V((1024, 768), F32), V((192, 768), LOW), V((192, 768), LOW),
         V((192, 768), LOW),
         dma((4,)), dma((8,)), dma((8,)), dma((4,)), dma((16, 4, 2)), dma((7,)), dma((7, 4)),
-        dma((7,)), dma((7,)), dma((7,)), dma((2, 2)), dma((2,)), dma((2,)),
+        dma((7,)), dma((7,)), dma((7,)), dma((2, 2)), dma((2, 4)), dma((2,)),
         dma((6,)), dma((6,)), dma((6,)),
     ]
     shapes = (

time: 131 us -> 127 us (0.969)
  Pallas kernels: 130 us -> 126 us
    pallas_call x1, Pallas kernels: 123 us -> 119 us  [kernel_call(): pl.pallas_call(step_kernel, out_shape=[jax.ShapeDtypeStruct(s, F32) for s...]
where the time goes in v5:
time: 127 us
  Pallas kernels  126 us (99%)
    pallas_call x1, Pallas kernels, kernel_call(): pl.pallas_call(step_kernel, out_shape=[jax.ShapeDtypeStruct(s, F32) for s...  119 us
    pallas_call x1, Pallas kernels, update_call(): pl.pallas_call(update_kernel, grid=(2,), out_shape=[like(g[0]) for g in (...  7.22 us

profile of v5, /device:TPU:0, one launch (start us, length us, event | category | flops | bytes accessed | tf_op | source)
XLA Modules:
  0.0 126.5 jit_solution(2606663678685523694)
XLA Ops:
  0.6 118.5 %shard_map.263 = (f32[2,24,3072]{2,1,0:T(8,128)}, f32[2,24,3072]{2,1,0:T(8,128)}, f32[2,96,768]{2,1,0:T(8,128)}, f32[2,8,128]{2,1,0:T(8,128)}, f32[512,768]{1,0:T(8,128)}, /*index=5*/f32[512,768]{1,0:T(8,128)}) custom-call(bf16[512,768]{1,0:T(8,128)(2,1)} %bitcast.5, bf16[512,768]{1,0:T(8,128)(2,1)} %bitcast.6, f32[2,24,3072]{2,1,0:T(8,128)} %refs_0_.1, ...), custom_call_target="tpu_custom_call" | custom-call | tf_op jit(solution)/shard_map/pallas_call | solution.py:1218
  119.2 7.2 %shard_map.264 = (f32[2,24,3072]{2,1,0:T(8,128)}, f32[2,24,3072]{2,1,0:T(8,128)}, f32[2,24,3072]{2,1,0:T(8,128)}, f32[2,24,3072]{2,1,0:T(8,128)}, f32[2,24,3072]...) custom-call(f32[2,24,3072]{2,1,0:T(8,128)} %refs_0_.1, ...), custom_call_target="tpu_custom_call" | custom-call | tf_op jit(solution)/shard_map/pallas_call | solution.py:1268

commit v6 on v5

--- a/solution.py
+++ b/solution.py
@@ -727,7 +727,7 @@
 
         from_slots(lambda s: R[s, m].astype(F32), write)
 
-    early_own = (0, 2, 3)
+    early_own = (0, 1, 2, 3)
 
     def gather_start(n):
         buf = gathered[n]
@@ -935,7 +935,6 @@
     Gb[...] = hidden.astype(LOW)
     P2s[...] = dot_nn(Gb[...], W2[...]).astype(LOW).reshape(16, 16, 768)
     sum_start(0)
-    direct(3, lambda t: m1s.at[t])
     sum_forward(0)
     hidden_sum = sum_done(0)
     second = normed + hidden_sum + vec(54)
@@ -952,6 +951,7 @@
     XH[core, own] = jnp.concatenate([hat_two, extra], axis=1).astype(LOW)
     gather_start(2)
     gather_forward(2)
+    direct(3, lambda t: m1s.at[t])
     gather_forward(1)
     gather_done(2)
     remote(XH.at[core], XH.at[core], sib_s.at[7], sib_r.at[7], sibling).start()

time: 127 us -> 124 us (0.976)
  Pallas kernels: 126 us -> 123 us
    pallas_call x1, Pallas kernels: 119 us -> 116 us  [kernel_call(): pl.pallas_call(step_kernel, out_shape=[jax.ShapeDtypeStruct(s, F32) for s...]
where the time goes in v6:
time: 124 us
  Pallas kernels  123 us (99%)
    pallas_call x1, Pallas kernels, kernel_call(): pl.pallas_call(step_kernel, out_shape=[jax.ShapeDtypeStruct(s, F32) for s...  116 us
    pallas_call x1, Pallas kernels, update_call(): pl.pallas_call(update_kernel, grid=(2,), out_shape=[like(g[0]) for g in (...  7.22 us

profile of v6, /device:TPU:0, one launch (start us, length us, event | category | flops | bytes accessed | tf_op | source)
XLA Modules:
  0.0 124.3 jit_solution(10506622904548380335)
XLA Ops:
  0.6 116.3 %shard_map.263 = (f32[2,24,3072]{2,1,0:T(8,128)}, f32[2,24,3072]{2,1,0:T(8,128)}, f32[2,96,768]{2,1,0:T(8,128)}, f32[2,8,128]{2,1,0:T(8,128)}, f32[512,768]{1,0:T(8,128)}, /*index=5*/f32[512,768]{1,0:T(8,128)}) custom-call(bf16[512,768]{1,0:T(8,128)(2,1)} %bitcast.5, bf16[512,768]{1,0:T(8,128)(2,1)} %bitcast.6, f32[2,24,3072]{2,1,0:T(8,128)} %refs_0_.1, ...), custom_call_target="tpu_custom_call" | custom-call | tf_op jit(solution)/shard_map/pallas_call | solution.py:1218
  116.9 7.2 %shard_map.264 = (f32[2,24,3072]{2,1,0:T(8,128)}, f32[2,24,3072]{2,1,0:T(8,128)}, f32[2,24,3072]{2,1,0:T(8,128)}, f32[2,24,3072]{2,1,0:T(8,128)}, f32[2,24,3072]...) custom-call(f32[2,24,3072]{2,1,0:T(8,128)} %refs_0_.1, ...), custom_call_target="tpu_custom_call" | custom-call | tf_op jit(solution)/shard_map/pallas_call | solution.py:1268

commit v7 on v6

--- a/solution.py
+++ b/solution.py
@@ -1067,9 +1067,9 @@
         m2s[slot] = pack(v)
 
     to_slots(lambda w: DX[w, 0:256], write_m2)
+    gather_forward(3)
     direct(6, lambda t: m2s.at[t])
     m2r[own] = m2s[own]
-    gather_forward(3)
 
     grad_cls = grad_one + dot_nt(grad_query, WN[0])
     cls_high, cls_rest = split_low(grad_cls)

time: 124 us -> 125 us (level)
  no operation moved by 1% of the time
where the time goes in v7:
time: 125 us
  Pallas kernels  124 us (99%)
    pallas_call x1, Pallas kernels, kernel_call(): pl.pallas_call(step_kernel, out_shape=[jax.ShapeDtypeStruct(s, F32) for s...  117 us
    pallas_call x1, Pallas kernels, update_call(): pl.pallas_call(update_kernel, grid=(2,), out_shape=[like(g[0]) for g in (...  7.22 us

profile of v7, /device:TPU:0, one launch (start us, length us, event | category | flops | bytes accessed | tf_op | source)
XLA Modules:
  0.0 124.7 jit_solution(13140287325663191674)
XLA Ops:
  0.6 116.7 %shard_map.263 = (f32[2,24,3072]{2,1,0:T(8,128)}, f32[2,24,3072]{2,1,0:T(8,128)}, f32[2,96,768]{2,1,0:T(8,128)}, f32[2,8,128]{2,1,0:T(8,128)}, f32[512,768]{1,0:T(8,128)}, /*index=5*/f32[512,768]{1,0:T(8,128)}) custom-call(bf16[512,768]{1,0:T(8,128)(2,1)} %bitcast.5, bf16[512,768]{1,0:T(8,128)(2,1)} %bitcast.6, f32[2,24,3072]{2,1,0:T(8,128)} %refs_0_.1, ...), custom_call_target="tpu_custom_call" | custom-call | tf_op jit(solution)/shard_map/pallas_call | solution.py:1218
  117.3 7.2 %shard_map.264 = (f32[2,24,3072]{2,1,0:T(8,128)}, f32[2,24,3072]{2,1,0:T(8,128)}, f32[2,24,3072]{2,1,0:T(8,128)}, f32[2,24,3072]{2,1,0:T(8,128)}, f32[2,24,3072]...) custom-call(f32[2,24,3072]{2,1,0:T(8,128)} %refs_0_.1, ...), custom_call_target="tpu_custom_call" | custom-call | tf_op jit(solution)/shard_map/pallas_call | solution.py:1268
